TPU v7x, 256 devices: a whole 4x4x8 slice. The times are simulated.
256 devices in a mesh: dp: 32 (over z, x), row: 2 (over core), col: 4 (over y).
Axes of the slice: x: 4, y: 4, z: 8, core: 2. Of those that a mesh axis runs over, the one named last changes fastest.
Arguments:
- weight: float32 [256, 24576], P(('row', 'dp'), 'col'), may hold values from -36 to 36, as said below
- momentum: float32 [256, 24576], P(('row', 'dp'), 'col'), may hold values from -1.5 to 1.5
- grad_parts: bfloat16 [32, 256, 24576], P('dp', 'row', 'col'), may hold values from -1.8 to 1.8, as said below
Outputs:
- new_weight: float32 [256, 24576], P(('row', 'dp'), 'col')
- new_momentum: float32 [256, 24576], P(('row', 'dp'), 'col')
Inputs may be any that keep to these rules, and one draw needn't show every extreme that they name: `weight`: entries of the matrix, finite. `grad_parts`: entries of the partials, finite.
All inputs are finite; a program needn't handle non-finite values.
Results may differ from a plain program's by a relative error of at most 0.0003.
Values sent between devices are 32-bit elements; how exact they have to be, the bound alone decides.
No kernel may reach another device: no remote copies, remote signals or barrier semaphores. Data moves between devices by JAX's collectives and lax.ppermute only.
A program may use at most 64 MiB of HBM per device.

v0:
```python
import jax
import jax.numpy as jnp
from jax import lax
from jax.sharding import PartitionSpec as P

clip_bound = 0.08
small_term = 1e-06
momentum_decay = 0.9
learn_rate = 1.0


def apply_update(weight, momentum, gradient, weight_sq, grad_sq):
    factor = jnp.minimum(1.0, clip_bound * jnp.sqrt(weight_sq) * lax.rsqrt(grad_sq + small_term))
    new_momentum = momentum_decay * momentum + factor[:, None] * gradient
    return (weight - learn_rate * new_momentum, new_momentum)


def sum_parts(grad_parts):
    local = grad_parts[0]
    gradient = lax.psum_scatter(local.astype(jnp.float32), "dp", scatter_dimension=0, tiled=True)
    return (gradient, jnp.sum(gradient * gradient, axis=1))


def per_device(weight, momentum, grad_parts):
    gradient, local_gsq = sum_parts(grad_parts)
    weight_sq, grad_sq = lax.psum((jnp.sum(weight * weight, axis=1), local_gsq), "col")
    new_weight, new_momentum = apply_update(weight, momentum, gradient, weight_sq, grad_sq)
    return (new_weight, new_momentum)


def solution(mesh):
    in_specs = (P(("row", "dp"), "col"), P(("row", "dp"), "col"), P("dp", "row", "col"))
    out_specs = (P(("row", "dp"), "col"), P(("row", "dp"), "col"))
    return jax.shard_map(
        per_device, mesh=mesh, in_specs=in_specs, out_specs=out_specs, check_vma=False
    )
```

profile of v0, /device:TPU:24, one launch (start us, length us, event | category | flops | bytes accessed | tf_op | source)
XLA Modules:
  0.0 189.6 jit_solution(16919747872199669157)
XLA Ops:
  7.2 0.0 copy-start.2
  7.2 0.0 copy-start
  7.2 0.0 copy-start.1
  7.2 0.0 all-reduce.4.cloned.1.call-start
  7.2 3.5 %bitcast_convert_fusion = f32[128,6144]{1,0:T(8,128)} fusion(bf16[1,128,6144]{2,1,0:T(8,128)(2,1)} %param.5), kind=kLoop, calls=%fused_computation | loop fusion | flops 786432 | bytes 4718592 | tf_op jit(solution)/shard_map/convert_element_type | solution.py:20
  10.7 0.0 all-reduce.4.cloned.1.call-update
  10.7 0.0 copy-done.2
  10.7 0.6 dynamic-slice
  12.0 0.0 copy-done
  12.0 0.2 multiply_reduce_fusion.1
  12.2 160.3 %all-reduce.4.cloned.1.call-done = f32[128,6144]{1,0:T(8,128)} async-done(((f32[128,6144]{1,0:T(8,128)}), f32[128,6144]{1,0:T(8,128)}) %all-reduce.4.cloned.1.call-update) | async-done | bytes 3145744
  172.5 1.1 multiply_reduce_fusion
  173.6 7.5 %all-reduce.1 = (f32[4]{0:T(128)S(1)}, f32[4]{0:T(128)S(1)}) all-reduce(f32[4]{0:T(128)S(1)} %multiply_reduce_fusion, f32[4]{0:T(128)S(1)} %multiply_reduce_fusion.1), channel_id=1, replica_groups=mesh['dp'=32,'row'=2,'col'=4] {'col'}, use_global_device_ids=true, to_apply=%region_4.0 | all-reduce | flops 8 | bytes 64 | tf_op jit(solution)/shard_map/psum | solution.py:26
  181.1 0.0 copy-done.1
  181.1 1.7 fusion
  (1 shorter events, 0.0 us)
Async XLA Ops:
  7.2 3.6 %copy-start.2 = (u32[256]{0:T(256)S(1)}, u32[256]{0:T(256)}, u32[]{:S(2)}) copy-start(u32[256]{0:T(256)} %constant.15) | copy-start | bytes 3076
  7.2 4.8 %copy-start = (f32[4,6144]{1,0:T(4,128)S(1)}, f32[4,6144]{1,0:T(4,128)}, u32[]{:S(2)}) copy-start(f32[4,6144]{1,0:T(4,128)} %param.3) | copy-start | bytes 294916
  7.2 173.9 %copy-start.1 = (f32[4,6144]{1,0:T(4,128)S(1)}, f32[4,6144]{1,0:T(4,128)}, u32[]{:S(2)}) copy-start(f32[4,6144]{1,0:T(4,128)} %param.4) | copy-start | bytes 294916
  7.2 165.3 %all-reduce.4.cloned.1.call-start = ((), (), s32[]{:S(2)}) async-start(), calls=%async_computation | async-start | bytes 6291456
Sparse Core Ops, SparseCore 0:
  11.5 160.9 all-reduce.3
where the time goes:
time: 192 us; the launch traced here: 190 us
  waiting for transfers between devices  160 us (83%)
  between operations  14.7 us (8%)
  blocking collectives  7.47 us (4%)
  other arithmetic  6.44 us (3%)
    unnamed x2, waiting for transfers between devices  160 us
    psum x1, blocking collectives, per_device(): lax.psum((jnp.sum(weight * weight, axis=1), local_gsq), 'col')  7.47 us
  transfers between devices with their start and end apart: 1, of which 1 were waited for; matrix products, arithmetic and copies ran while one was open for 0% of the time, Pallas kernels for 0%

commit v1 on v0

v1 whole, which is shorter than its diff:
```python
import jax
import jax.numpy as jnp
from jax import lax
from jax.sharding import PartitionSpec as P

clip_bound = 0.08
small_term = 1e-06
momentum_decay = 0.9
learn_rate = 1.0

NZ, NX, NY, NCORE = 8, 4, 4, 2
SPLIT = 3072


def pairs_zx(target):
    out = []
    for z in range(NZ):
        for x in range(NX):
            for core in range(NCORE):
                tz, tx = target(z, x, core)
                out.append((((z * NX + x) * NCORE + core), ((tz % NZ) * NX + tx) * NCORE + core))
    return out


def sign(z, core):
    return 2 * ((z + core) % 2) - 1


def x_first(core):
    return 1 + 2 * core


def x_second(core):
    return 3 - 2 * core


def send(value, target):
    return lax.ppermute(value, ("dp", "row"), pairs_zx(target))


def send_x_first(value):
    return send(value, lambda z, x, core: (z, x ^ x_first(core)))


def send_x_second(value):
    return send(value, lambda z, x, core: (z, x ^ x_second(core)))


def send_z_pair(value):
    return send(value, lambda z, x, core: (z - sign(z, core), x))


def send_z_far(value, k):
    return send(value, lambda z, x, core: (z + sign(z, core) * k, x))


def pick(value, index, axis):
    return lax.dynamic_index_in_dim(value, index, axis, keepdims=False)


def sum_parts(local):
    cols = local.shape[1]
    cut = min(SPLIT, cols // 2)
    dp = lax.axis_index("dp")
    core = lax.axis_index("row")
    z, x = dp // NX, dp % NX
    s = 2 * ((z + core) % 2) - 1
    m1, m2, diag = x ^ (1 + 2 * core), x ^ (3 - 2 * core), x ^ 2
    keep_z = [(z + s * k + NZ) % NZ for k in range(4)]
    give_z = [(z - s * (1 + k) + NZ) % NZ for k in range(4)]

    f32 = jnp.float32
    a = local[:, :cut].reshape(NZ, NX, 4, cut)
    b = local[:, cut:].reshape(NZ, NX, 4, cols - cut)

    a_got = send_x_first(jnp.stack([pick(a, m1, 1), pick(a, diag, 1)]).astype(f32))
    b_got = send_z_pair(jnp.stack([pick(b, i, 0) for i in give_z]).astype(f32))
    a_out = pick(a, m2, 1).astype(f32) + a_got[1]
    a_got2 = send_x_second(a_out)
    b_sum = jnp.stack([pick(b, i, 0) for i in keep_z]).astype(f32) + b_got
    b_got2 = send_x_first(jnp.stack([pick(b_sum, m1, 1), pick(b_sum, diag, 1)]))
    a_sum = pick(a, x, 1).astype(f32) + a_got[0] + a_got2
    a_got3 = send_z_pair(jnp.stack([pick(a_sum, i, 0) for i in give_z]))
    b_got3 = send_x_second(pick(b_sum, m2, 1) + b_got2[1])
    a_sum = jnp.stack([pick(a_sum, i, 0) for i in keep_z]) + a_got3
    b_sum = pick(b_sum, x, 1) + b_got2[0] + b_got3
    far = [send_z_far(jnp.concatenate([a_sum[k], b_sum[k]], axis=1), k) for k in (1, 2, 3)]
    return jnp.concatenate([a_sum[0], b_sum[0]], axis=1) + far[0] + far[1] + far[2]


def sum_over_col(value):
    value = value + lax.ppermute(value, "col", [(i, i ^ 1) for i in range(NY)])
    return value + lax.ppermute(value, "col", [(i, i ^ 3) for i in range(NY)])


def per_device(weight, momentum, grad_parts):
    weight_sq = sum_over_col(jnp.sum(weight * weight, axis=1, keepdims=True))
    gradient = sum_parts(grad_parts[0])
    grad_sq = sum_over_col(jnp.sum(gradient * gradient, axis=1, keepdims=True))
    factor = jnp.minimum(1.0, clip_bound * jnp.sqrt(weight_sq) * lax.rsqrt(grad_sq + small_term))
    new_momentum = momentum_decay * momentum + factor * gradient
    return (weight - learn_rate * new_momentum, new_momentum)


def solution(mesh):
    in_specs = (P(("row", "dp"), "col"), P(("row", "dp"), "col"), P("dp", "row", "col"))
    out_specs = (P(("row", "dp"), "col"), P(("row", "dp"), "col"))
    return jax.shard_map(
        per_device, mesh=mesh, in_specs=in_specs, out_specs=out_specs, check_vma=False
    )
```

time: 192 us -> 63 us (0.33); the launches traced: 190 us -> 62.8 us
  waiting for transfers between devices: 160 us -> 28.6 us
  starting transfers between devices: 0.04 us -> 26.1 us
  between operations: 14.7 us -> 1.02 us
  blocking collectives: 7.47 us -> 0 us
  local copies, waits for them, and re-layouts: 0.6 us -> 3.3 us
  other arithmetic: 6.44 us -> 3.78 us
    unnamed x2 -> x0, waiting for transfers between devices: 160 us -> none
    ppermute x0 -> x13, waiting for transfers between devices: none -> 28.6 us  [the longest x9 21.3 us: send(): return lax.ppermute(value, ('dp', 'row'), pairs_zx(target))]
    ppermute x0 -> x13, starting transfers between devices: none -> 26.1 us  [the longest x9 24 us: send(): return lax.ppermute(value, ('dp', 'row'), pairs_zx(target))]
    psum x1 -> x0, blocking collectives: 7.47 us -> none  [per_device(): lax.psum((jnp.sum(weight * weight, axis=1), local_gsq), 'col')]
    convert_element_type x1 -> x2, other arithmetic: 3.46 us -> 0.52 us  [the longest x1 0.27 us: sum_parts(): b_got = send_z_pair(jnp.stack([pick(b, i, 0) for i in give_z]).astype(f32))]
    add x0 -> x8, other arithmetic: none -> 1.92 us  [the longest x1 1.47 us: sum_parts(): b_sum = jnp.stack([pick(b, i, 0) for i in keep_z]).astype(f32) + b_got]
  transfers between devices with their start and end apart: 1 -> 13, of which waited for: 1 -> 8; matrix products, arithmetic and copies ran while one was open for 0% -> 5% of each run, Pallas kernels for 0% -> 0%
where the time goes in v1:
time: 63 us; the launch traced here: 62.8 us
  waiting for transfers between devices  28.6 us (45%)
  starting transfers between devices  26.1 us (41%)
  other arithmetic  3.78 us (6%)
  local copies, waits for them, and re-layouts  3.3 us (5%)
  between operations  1.02 us (2%)
    ppermute x9, starting transfers between devices, send(): return lax.ppermute(value, ('dp', 'row'), pairs_zx(target))  24 us
    ppermute x9, waiting for transfers between devices, send(): return lax.ppermute(value, ('dp', 'row'), pairs_zx(target))  21.3 us
    ppermute x2, waiting for transfers between devices, sum_over_col(): return value + lax.ppermute(value, 'col', [(i, i ^ 3) for i in range(NY)])  4.53 us
    ppermute x2, waiting for transfers between devices, sum_over_col(): value = value + lax.ppermute(value, 'col', [(i, i ^ 1) for i in range(NY)])  2.8 us
    ppermute x2, starting transfers between devices, sum_over_col(): value = value + lax.ppermute(value, 'col', [(i, i ^ 1) for i in range(NY)])  1.65 us
    slice x1, local copies, waits for them, and re-layouts, sum_parts(): a = local[:, :cut].reshape(NZ, NX, 4, cut)  1.47 us
    add x1, other arithmetic, sum_parts(): b_sum = jnp.stack([pick(b, i, 0) for i in keep_z]).astype(f32) + b_got  1.47 us
  transfers between devices with their start and end apart: 13, of which 8 were waited for; matrix products, arithmetic and copies ran while one was open for 5% of the time, Pallas kernels for 0%

profile of v1, /device:TPU:24, one launch (start us, length us, event | category | flops | bytes accessed | tf_op | source)
XLA Modules:
  0.0 62.8 jit_solution(9497878958155555313)
XLA Ops:
  0.8 1.5 %fusion.10 = (bf16[128,3072]{1,0:T(8,128)(2,1)S(1)}, bf16[128,3072]{1,0:T(8,128)(2,1)S(1)}) fusion(bf16[128,6144]{1,0:T(8,128)(2,1)} %bitcast.79), kind=kLoop, calls=%fused_computation.57 | loop fusion | bytes 3145728 | tf_op jit(solution)/shard_map/slice | solution.py:73
  2.3 0.3 reshape.19
  2.6 1.0 %dynamic-slice_bitcast_fusion.11 = (bf16[1,4,4,3072]{3,2,0,1:T(4,128)(2,1)S(1)}, bf16[1,4,4,3072]{3,2,0,1:T(4,128)(2,1)S(1)}, bf16[1,4,4,3072]{3,2,0,1:T(4,128)(...) fusion(bf16[8,4,4,3072]{3,2,1,0:T(4,128)(2,1)S(1)} %reshape.19,, ...), kind=kLoop, calls=%fused_computation.35 | loop fusion | bytes 1572896
  3.6 0.3 maximum_convert_fusion.1
  3.9 2.0 %collective-permute-start.5 = (f32[4,4,4,3072]{3,2,0,1:T(4,128)S(1)}, f32[4,4,4,3072]{3,2,0,1:T(4,128)}, u32[]{:S(2)}, u32[]{:S(2)}) collective-permute-start(f32[4,4,4,3072]{3,2,0,1:T(4,128)S(1)} %maximum_convert_fusion.1), channel_id=1, source_target_pairs={{0,32},{4,228},{8,40},{12,236},{16,48},{20,244},{24,56},{28,252},{... | collective-permute-start | bytes 2359304 | tf_op jit(solution)/shard_map/ppermute | solution.py:38
  5.9 0.0 copy-start
  5.9 0.3 reshape.18
  6.2 0.1 dynamic-slice_bitcast_fusion.3
  6.4 0.2 maximum_convert_fusion
  6.6 1.6 %collective-permute-start.2 = (f32[2,8,4,3072]{3,2,1,0:T(4,128)S(1)}, f32[2,8,4,3072]{3,2,1,0:T(4,128)S(1)}, u32[]{:S(2)}, u32[]{:S(2)}) collective-permute-start(f32[2,8,4,3072]{3,2,1,0:T(4,128)S(1)} %maximum_convert_fusion), channel_id=1, source_target_pairs={{0,8},{4,28},{8,0},{12,20},{16,24},{20,12},{24,16},{28,4},{32,40},... | collective-permute-start | bytes 2359304 | tf_op jit(solution)/shard_map/ppermute | solution.py:38
  8.2 0.0 copy-done
  8.2 0.2 multiply_reduce_fusion.1
  8.4 0.8 %collective-permute-start = (f32[4,1]{0,1:T(1,128)S(1)}, f32[4,1]{0,1:T(1,128)S(1)}, u32[]{:S(2)}, u32[]{:S(2)}) collective-permute-start(f32[4,1]{0,1:T(1,128)S(1)} %bitcast.80), channel_id=1, source_target_pairs={{0,1},{1,0},{2,3},{3,2},{4,5},{5,4},{6,7},{7,6},{8,9},{9,8},{10,11... | collective-permute-start | bytes 56 | tf_op jit(solution)/shard_map/ppermute | solution.py:92
  9.2 6.9 %collective-permute-done.5 = f32[4,4,4,3072]{3,2,0,1:T(4,128)} collective-permute-done((f32[4,4,4,3072]{3,2,0,1:T(4,128)S(1)}, f32[4,4,4,3072]{3,2,0,1:T(4,128)}, u32[]{:S(2)}, u32[]{:S(2)}) %collective-permute-start.5) | collective-permute-done | bytes 786464 | tf_op jit(solution)/shard_map/ppermute | solution.py:38
  16.1 1.5 %convert_add_fusion = f32[4,4,4,3072]{3,2,0,1:T(4,128)S(1)} fusion(f32[4,4,4,3072]{3,2,0,1:T(4,128)} %collective-permute-done.5, bf16[1,4,4,3072]{3,2,0,1:T(4,128)(2,1)S(1)} %get-tuple-element.16, bf16[1,4,4,3072]{3,2,0,1:T(4,128)(2,1)S(1)} %get-tuple-element.17, bf16[1,4,4,3072]{3,2,0,1:T(4,128)(2,1)} %get-tuple-element.18, ...), kind=kLoop, calls=%fused_computation | loop fusion | flops 983040 | bytes 1966080 | tf_op jit(solution)/shard_map/add | solution.py:80
  17.6 0.1 pad_maximum_fusion
  17.7 1.6 %collective-permute-start.6 = (f32[2,4,4,3072]{3,2,1,0:T(4,128)S(1)}, f32[2,4,4,3072]{3,2,1,0:T(4,128)S(1)}, u32[]{:S(2)}, u32[]{:S(2)}) collective-permute-start(f32[2,4,4,3072]{3,2,1,0:T(4,128)S(1)} %pad_maximum_fusion), channel_id=1, source_target_pairs={{0,8},{4,28},{8,0},{12,20},{16,24},{20,12},{24,16},{28,4},{32,40},... | collective-permute-start | bytes 1179656 | tf_op jit(solution)/shard_map/ppermute | solution.py:38
  19.3 0.0 collective-permute-done.2
  19.3 0.1 fusion
  19.4 2.3 %collective-permute-start.3 = (f32[8,4,3072]{2,1,0:T(4,128)S(1)}, f32[8,4,3072]{2,1,0:T(4,128)S(1)}, u32[]{:S(2)}, u32[]{:S(2)}) collective-permute-start(f32[8,4,3072]{2,1,0:T(4,128)S(1)} %fusion), channel_id=1, source_target_pairs={{0,24},{4,12},{8,16},{12,4},{16,8},{20,28},{24,0},{28,20},{32,56},... | collective-permute-start | bytes 1179656 | tf_op jit(solution)/shard_map/ppermute | solution.py:38
  21.6 3.9 %collective-permute-done.6 = f32[2,4,4,3072]{3,2,1,0:T(4,128)S(1)} collective-permute-done((f32[2,4,4,3072]{3,2,1,0:T(4,128)S(1)}, f32[2,4,4,3072]{3,2,1,0:T(4,128)S(1)}, u32[]{:S(2)}, u32[]{:S(2)}) %collective-permute-start.6) | collective-permute-done | bytes 393248 | tf_op jit(solution)/shard_map/ppermute | solution.py:38
  25.6 0.1 fusion.3
  25.6 3.3 %collective-permute-start.7 = (f32[4,4,3072]{2,1,0:T(4,128)S(1)}, f32[4,4,3072]{2,1,0:T(4,128)S(1)}, u32[]{:S(2)}, u32[]{:S(2)}) collective-permute-start(f32[4,4,3072]{2,1,0:T(4,128)S(1)} %fusion.3), channel_id=1, source_target_pairs={{0,24},{4,12},{8,16},{12,4},{16,8},{20,28},{24,0},{28,20},{32,56},... | collective-permute-start | bytes 589832 | tf_op jit(solution)/shard_map/ppermute | solution.py:38
  28.9 3.6 %collective-permute-done.3 = f32[8,4,3072]{2,1,0:T(4,128)S(1)} collective-permute-done((f32[8,4,3072]{2,1,0:T(4,128)S(1)}, f32[8,4,3072]{2,1,0:T(4,128)S(1)}, u32[]{:S(2)}, u32[]{:S(2)}) %collective-permute-start.3) | collective-permute-done | bytes 393248 | tf_op jit(solution)/shard_map/ppermute | solution.py:38
  32.5 0.1 fusion.2
  32.8 0.0 copy-start.1
  32.8 2.1 %collective-permute-start.4 = (f32[4,4,3072]{2,1,0:T(4,128)S(1)}, f32[4,4,3072]{2,1,0:T(4,128)S(1)}, u32[]{:S(2)}, u32[]{:S(2)}) collective-permute-start(f32[4,4,3072]{2,1,0:T(4,128)S(1)} %pad_maximum_fusion.1), channel_id=1, source_target_pairs={{0,32},{4,228},{8,40},{12,236},{16,48},{20,244},{24,56},{28,252},{... | collective-permute-start | bytes 589832 | tf_op jit(solution)/shard_map/ppermute | solution.py:38
  34.9 0.0 collective-permute-done.7
  34.9 0.1 fusion.5
  35.0 3.5 %collective-permute-done.4 = f32[4,4,3072]{2,1,0:T(4,128)S(1)} collective-permute-done((f32[4,4,3072]{2,1,0:T(4,128)S(1)}, f32[4,4,3072]{2,1,0:T(4,128)S(1)}, u32[]{:S(2)}, u32[]{:S(2)}) %collective-permute-start.4) | collective-permute-done | bytes 196640 | tf_op jit(solution)/shard_map/ppermute | solution.py:38
  38.6 0.1 maximum_add_fusion
  38.7 5.8 %collective-permute-start.10 = (f32[4,6144]{1,0:T(4,128)S(1)}, f32[4,6144]{1,0:T(4,128)S(1)}, u32[]{:S(2)}, u32[]{:S(2)}) collective-permute-start(f32[4,6144]{1,0:T(4,128)S(1)} %pad_maximum_fusion.4), channel_id=1, source_target_pairs={{0,160},{4,100},{8,168},{12,108},{16,176},{20,116},{24,184},{28,12... | collective-permute-start | bytes 294920 | tf_op jit(solution)/shard_map/ppermute | solution.py:38
  44.6 0.8 %collective-permute-start.9 = (f32[4,6144]{1,0:T(4,128)S(1)}, f32[4,6144]{1,0:T(4,128)S(1)}, u32[]{:S(2)}, u32[]{:S(2)}) collective-permute-start(f32[4,6144]{1,0:T(4,128)S(1)} %pad_maximum_fusion.3), channel_id=1, source_target_pairs={{0,192},{4,68},{8,200},{12,76},{16,208},{20,84},{24,216},{28,92},{... | collective-permute-start | bytes 294920 | tf_op jit(solution)/shard_map/ppermute | solution.py:38
  45.4 4.6 %collective-permute-start.8 = (f32[4,6144]{1,0:T(4,128)S(1)}, f32[4,6144]{1,0:T(4,128)S(1)}, u32[]{:S(2)}, u32[]{:S(2)}) collective-permute-start(f32[4,6144]{1,0:T(4,128)S(1)} %pad_maximum_fusion.2), channel_id=1, source_target_pairs={{0,224},{4,36},{8,232},{12,44},{16,240},{20,52},{24,248},{28,60},{... | collective-permute-start | bytes 294920 | tf_op jit(solution)/shard_map/ppermute | solution.py:38
  49.9 0.0 collective-permute-done
  49.9 0.2 collective-permute-start.1
  50.2 0.0 collective-permute-done.10
  50.2 1.6 %collective-permute-done.9 = f32[4,6144]{1,0:T(4,128)S(1)} collective-permute-done((f32[4,6144]{1,0:T(4,128)S(1)}, f32[4,6144]{1,0:T(4,128)S(1)}, u32[]{:S(2)}, u32[]{:S(2)}) %collective-permute-start.9) | collective-permute-done | bytes 98336 | tf_op jit(solution)/shard_map/ppermute | solution.py:38
  51.8 1.7 %collective-permute-done.8 = f32[4,6144]{1,0:T(4,128)S(1)} collective-permute-done((f32[4,6144]{1,0:T(4,128)S(1)}, f32[4,6144]{1,0:T(4,128)S(1)}, u32[]{:S(2)}, u32[]{:S(2)}) %collective-permute-start.8) | collective-permute-done | bytes 98336 | tf_op jit(solution)/shard_map/ppermute | solution.py:38
  53.5 0.2 multiply_reduce_fusion
  53.6 0.8 %collective-permute-start.11 = (f32[4,1]{0,1:T(1,128)S(1)}, f32[4,1]{0,1:T(1,128)S(1)}, u32[]{:S(2)}, u32[]{:S(2)}) collective-permute-start(f32[4,1]{0,1:T(1,128)S(1)} %bitcast.81), channel_id=1, source_target_pairs={{0,1},{1,0},{2,3},{3,2},{4,5},{5,4},{6,7},{7,6},{8,9},{9,8},{10,11... | collective-permute-start | bytes 56 | tf_op jit(solution)/shard_map/ppermute | solution.py:92
  54.5 2.8 %collective-permute-done.11 = f32[4,1]{0,1:T(1,128)S(1)} collective-permute-done((f32[4,1]{0,1:T(1,128)S(1)}, f32[4,1]{0,1:T(1,128)S(1)}, u32[]{:S(2)}, u32[]{:S(2)}) %collective-permute-start.11) | collective-permute-done | bytes 48 | tf_op jit(solution)/shard_map/ppermute | solution.py:92
  57.3 0.2 collective-permute-start.12
  57.5 0.0 collective-permute-done.1
  57.5 4.5 %collective-permute-done.12 = f32[4,1]{0,1:T(1,128)S(1)} collective-permute-done((f32[4,1]{0,1:T(1,128)S(1)}, f32[4,1]{0,1:T(1,128)S(1)}, u32[]{:S(2)}, u32[]{:S(2)}) %collective-permute-start.12) | collective-permute-done | bytes 48 | tf_op jit(solution)/shard_map/ppermute | solution.py:93
  62.0 0.0 copy-done.1
  62.0 0.8 %fusion.8 = (f32[4,6144]{1,0:T(4,128)}, f32[4,6144]{1,0:T(4,128)}) fusion(f32[4,6144]{1,0:T(4,128)S(1)} %copy-done, f32[4,6144]{1,0:T(4,128)S(1)} %get-tuple-element.5, f32[4]{0:T(128)S(1)} %minimum_bitcast_fusion, f32[4,6144]{1,0:T(4,128)S(1)} %copy-done.1), kind=kLoop, calls=%fused_computation.56 | loop fusion | flops 98304 | bytes 491536 | tf_op jit(solution)/shard_map/sub | solution.py:102
  (11 shorter events, 0.3 us)
Async XLA Ops:
  3.9 12.2 %collective-permute-start.5 = (f32[4,4,4,3072]{3,2,0,1:T(4,128)S(1)}, f32[4,4,4,3072]{3,2,0,1:T(4,128)}, u32[]{:S(2)}, u32[]{:S(2)}) collective-permute-start(f32[4,4,4,3072]{3,2,0,1:T(4,128)S(1)} %maximum_convert_fusion.1), channel_id=1, source_target_pairs={{0,32},{4,228},{8,40},{12,236},{16,48},{20,244},{24,56},{28,252},{... | collective-permute-start | bytes 2359304 | tf_op jit(solution)/shard_map/ppermute | solution.py:38
  5.9 2.3 %copy-start = (f32[4,6144]{1,0:T(4,128)S(1)}, f32[4,6144]{1,0:T(4,128)}, u32[]{:S(2)}) copy-start(f32[4,6144]{1,0:T(4,128)} %param.3) | copy-start | bytes 294916
  6.6 12.7 %collective-permute-start.2 = (f32[2,8,4,3072]{3,2,1,0:T(4,128)S(1)}, f32[2,8,4,3072]{3,2,1,0:T(4,128)S(1)}, u32[]{:S(2)}, u32[]{:S(2)}) collective-permute-start(f32[2,8,4,3072]{3,2,1,0:T(4,128)S(1)} %maximum_convert_fusion), channel_id=1, source_target_pairs={{0,8},{4,28},{8,0},{12,20},{16,24},{20,12},{24,16},{28,4},{32,40},... | collective-permute-start | bytes 2359304 | tf_op jit(solution)/shard_map/ppermute | solution.py:38
  8.4 41.6 %collective-permute-start = (f32[4,1]{0,1:T(1,128)S(1)}, f32[4,1]{0,1:T(1,128)S(1)}, u32[]{:S(2)}, u32[]{:S(2)}) collective-permute-start(f32[4,1]{0,1:T(1,128)S(1)} %bitcast.80), channel_id=1, source_target_pairs={{0,1},{1,0},{2,3},{3,2},{4,5},{5,4},{6,7},{7,6},{8,9},{9,8},{10,11... | collective-permute-start | bytes 56 | tf_op jit(solution)/shard_map/ppermute | solution.py:92
  17.7 7.9 %collective-permute-start.6 = (f32[2,4,4,3072]{3,2,1,0:T(4,128)S(1)}, f32[2,4,4,3072]{3,2,1,0:T(4,128)S(1)}, u32[]{:S(2)}, u32[]{:S(2)}) collective-permute-start(f32[2,4,4,3072]{3,2,1,0:T(4,128)S(1)} %pad_maximum_fusion), channel_id=1, source_target_pairs={{0,8},{4,28},{8,0},{12,20},{16,24},{20,12},{24,16},{28,4},{32,40},... | collective-permute-start | bytes 1179656 | tf_op jit(solution)/shard_map/ppermute | solution.py:38
  19.4 13.2 %collective-permute-start.3 = (f32[8,4,3072]{2,1,0:T(4,128)S(1)}, f32[8,4,3072]{2,1,0:T(4,128)S(1)}, u32[]{:S(2)}, u32[]{:S(2)}) collective-permute-start(f32[8,4,3072]{2,1,0:T(4,128)S(1)} %fusion), channel_id=1, source_target_pairs={{0,24},{4,12},{8,16},{12,4},{16,8},{20,28},{24,0},{28,20},{32,56},... | collective-permute-start | bytes 1179656 | tf_op jit(solution)/shard_map/ppermute | solution.py:38
  25.6 9.3 %collective-permute-start.7 = (f32[4,4,3072]{2,1,0:T(4,128)S(1)}, f32[4,4,3072]{2,1,0:T(4,128)S(1)}, u32[]{:S(2)}, u32[]{:S(2)}) collective-permute-start(f32[4,4,3072]{2,1,0:T(4,128)S(1)} %fusion.3), channel_id=1, source_target_pairs={{0,24},{4,12},{8,16},{12,4},{16,8},{20,28},{24,0},{28,20},{32,56},... | collective-permute-start | bytes 589832 | tf_op jit(solution)/shard_map/ppermute | solution.py:38
  32.8 29.2 %copy-start.1 = (f32[4,6144]{1,0:T(4,128)S(1)}, f32[4,6144]{1,0:T(4,128)}, u32[]{:S(2)}) copy-start(f32[4,6144]{1,0:T(4,128)} %param.4) | copy-start | bytes 294916
  32.8 5.8 %collective-permute-start.4 = (f32[4,4,3072]{2,1,0:T(4,128)S(1)}, f32[4,4,3072]{2,1,0:T(4,128)S(1)}, u32[]{:S(2)}, u32[]{:S(2)}) collective-permute-start(f32[4,4,3072]{2,1,0:T(4,128)S(1)} %pad_maximum_fusion.1), channel_id=1, source_target_pairs={{0,32},{4,228},{8,40},{12,236},{16,48},{20,244},{24,56},{28,252},{... | collective-permute-start | bytes 589832 | tf_op jit(solution)/shard_map/ppermute | solution.py:38
  38.7 11.4 %collective-permute-start.10 = (f32[4,6144]{1,0:T(4,128)S(1)}, f32[4,6144]{1,0:T(4,128)S(1)}, u32[]{:S(2)}, u32[]{:S(2)}) collective-permute-start(f32[4,6144]{1,0:T(4,128)S(1)} %pad_maximum_fusion.4), channel_id=1, source_target_pairs={{0,160},{4,100},{8,168},{12,108},{16,176},{20,116},{24,184},{28,12... | collective-permute-start | bytes 294920 | tf_op jit(solution)/shard_map/ppermute | solution.py:38
  44.6 7.2 %collective-permute-start.9 = (f32[4,6144]{1,0:T(4,128)S(1)}, f32[4,6144]{1,0:T(4,128)S(1)}, u32[]{:S(2)}, u32[]{:S(2)}) collective-permute-start(f32[4,6144]{1,0:T(4,128)S(1)} %pad_maximum_fusion.3), channel_id=1, source_target_pairs={{0,192},{4,68},{8,200},{12,76},{16,208},{20,84},{24,216},{28,92},{... | collective-permute-start | bytes 294920 | tf_op jit(solution)/shard_map/ppermute | solution.py:38
  45.4 8.1 %collective-permute-start.8 = (f32[4,6144]{1,0:T(4,128)S(1)}, f32[4,6144]{1,0:T(4,128)S(1)}, u32[]{:S(2)}, u32[]{:S(2)}) collective-permute-start(f32[4,6144]{1,0:T(4,128)S(1)} %pad_maximum_fusion.2), channel_id=1, source_target_pairs={{0,224},{4,36},{8,232},{12,44},{16,240},{20,52},{24,248},{28,60},{... | collective-permute-start | bytes 294920 | tf_op jit(solution)/shard_map/ppermute | solution.py:38
  49.9 7.5 %collective-permute-start.1 = (f32[4,1]{0,1:T(1,128)S(1)}, f32[4,1]{0,1:T(1,128)S(1)}, u32[]{:S(2)}, u32[]{:S(2)}) collective-permute-start(f32[4,1]{0,1:T(1,128)S(1)} %bitcast_add_fusion.1), channel_id=1, source_target_pairs={{0,3},{1,2},{2,1},{3,0},{4,7},{5,6},{6,5},{7,4},{8,11},{9,10},{10,... | collective-permute-start | bytes 56 | tf_op jit(solution)/shard_map/ppermute | solution.py:93
  53.6 3.6 %collective-permute-start.11 = (f32[4,1]{0,1:T(1,128)S(1)}, f32[4,1]{0,1:T(1,128)S(1)}, u32[]{:S(2)}, u32[]{:S(2)}) collective-permute-start(f32[4,1]{0,1:T(1,128)S(1)} %bitcast.81), channel_id=1, source_target_pairs={{0,1},{1,0},{2,3},{3,2},{4,5},{5,4},{6,7},{7,6},{8,9},{9,8},{10,11... | collective-permute-start | bytes 56 | tf_op jit(solution)/shard_map/ppermute | solution.py:92
  57.3 4.8 %collective-permute-start.12 = (f32[4,1]{0,1:T(1,128)S(1)}, f32[4,1]{0,1:T(1,128)S(1)}, u32[]{:S(2)}, u32[]{:S(2)}) collective-permute-start(f32[4,1]{0,1:T(1,128)S(1)} %bitcast_add_fusion), channel_id=1, source_target_pairs={{0,3},{1,2},{2,1},{3,0},{4,7},{5,6},{6,5},{7,4},{8,11},{9,10},{10,... | collective-permute-start | bytes 56 | tf_op jit(solution)/shard_map/ppermute | solution.py:93

commit v2 on v1

v2 whole, which is shorter than its diff:
```python
import functools

import jax
import jax.numpy as jnp
from jax import lax
from jax.experimental import pallas as pl
from jax.experimental.pallas import tpu as pltpu
from jax.sharding import PartitionSpec as P

clip_bound = 0.08
small_term = 1e-06
momentum_decay = 0.9
learn_rate = 1.0

NZ, NX, NY, NCORE = 8, 4, 4, 2
SHARE, TOTAL = 1, 2
CHUNK = 512
ORDER = (1, 2, 3)
COL_ORDER = (1, 3, 2)


def pairs_zx(target):
    out = []
    for z in range(NZ):
        for x in range(NX):
            for core in range(NCORE):
                tz, tx = target(z, x, core)
                out.append((((z * NX + x) * NCORE + core), ((tz % NZ) * NX + tx) * NCORE + core))
    return out


def sign(z, core):
    return 2 * ((z + core) % 2) - 1


def send(value, target):
    return lax.ppermute(value, ("dp", "row"), pairs_zx(target))


def send_x_first(value):
    return send(value, lambda z, x, core: (z, x ^ (1 + 2 * core)))


def send_x_second(value):
    return send(value, lambda z, x, core: (z, x ^ (3 - 2 * core)))


def send_z_pair(value):
    return send(value, lambda z, x, core: (z - sign(z, core), x))


def send_z_far(value, k):
    return send(value, lambda z, x, core: (z + sign(z, core) * k, x))


def pick(value, index, axis):
    return lax.dynamic_index_in_dim(value, index, axis, keepdims=False)


def place():
    dp, core = lax.axis_index("dp"), lax.axis_index("row")
    z, x = lax.div(dp, NX), lax.rem(dp, NX)
    return z, x, core, 2 * lax.rem(z + core, 2) - 1


def x_high(x, core):
    h = lax.broadcasted_iota(jnp.int32, (8, 1), 0) // 4
    return (lax.div(x, 2) ^ jnp.where((h != lax.rem(x, 2)) & (core == 0), 1, 0)) == 1


def z_high(z, s, j):
    return (z + s * (((j - z) * s) & 3)) & 7 >= 4


def each_chunk(cols, body):
    n = CHUNK if cols % CHUNK == 0 else 128
    lax.fori_loop(0, cols // n, lambda i, c: (body(pl.multiple_of(i * n, n), n), c)[1], 0)


def give_z_kernel(cut, src, out, buf, sem):
    z, x, core, s = place()
    copies = []
    for j in range(4):
        row = pl.multiple_of(jnp.where(z_high(z, s, j), 0, 64) + j * 16, 16)
        copies.append(pltpu.make_async_copy(src.at[pl.ds(row, 16), pl.ds(cut, buf.shape[2])], buf.at[j], sem.at[j]))
    for copy in copies:
        copy.start()
    for copy in copies:
        copy.wait()

    def body(first, n):
        for j in range(4):
            here = (j, slice(None), pl.ds(first, n))
            out[here] = buf[here].astype(jnp.float32)

    each_chunk(buf.shape[2], body)


def give_x_kernel(cut, src, out, buf, sem):
    z, x, core, s = place()
    copies = [
        pltpu.make_async_copy(src.at[pl.ds(j * 32, 32), pl.ds(0, cut)], buf.at[j], sem.at[j]) for j in range(4)
    ]
    for copy in copies:
        copy.start()
    for copy in copies:
        copy.wait()

    def body(first, n):
        high = jnp.broadcast_to(jnp.where(x_high(x, core), 1, 0), (8, n)) == 0
        for k in range(NZ):
            rows = buf[k // 2, k % 2 * 16 : k % 2 * 16 + 16, pl.ds(first, n)].astype(jnp.float32)
            out[k, :, pl.ds(first, n)] = jnp.where(high, rows[8:], rows[:8])

    each_chunk(cut, body)


def b_kernel(cut, src, got, own, out, buf, sem):
    z, x, core, s = place()
    copies = []
    for j in range(4):
        row = pl.multiple_of(jnp.where(z_high(z, s, j), 64, 0) + j * 16, 16)
        copies.append(pltpu.make_async_copy(src.at[pl.ds(row, 16), pl.ds(cut, buf.shape[2])], buf.at[j], sem.at[j]))
    for copy in copies:
        copy.start()
    for copy in copies:
        copy.wait()

    def body(first, n):
        cols = pl.ds(first, n)
        high = jnp.broadcast_to(jnp.where(x_high(x, core), 1, 0), (8, n)) == 1
        for j in range(4):
            rows = buf[j, :, cols].astype(jnp.float32) + got[j, :, cols]
            own[j * 8 : j * 8 + 8, cols] = jnp.where(high, rows[8:], rows[:8])
            out[j * 8 : j * 8 + 8, cols] = jnp.where(high, rows[:8], rows[8:])

    each_chunk(buf.shape[2], body)


def a_kernel(cut, src, got, own, out, buf, sem):
    z, x, core, s = place()
    copies = [
        pltpu.make_async_copy(src.at[pl.ds(j * 32, 32), pl.ds(0, cut)], buf.at[j], sem.at[j]) for j in range(4)
    ]
    for copy in copies:
        copy.start()
    for copy in copies:
        copy.wait()

    def body(first, n):
        cols = pl.ds(first, n)
        high = jnp.broadcast_to(jnp.where(x_high(x, core), 1, 0), (8, n)) == 1
        for j in range(4):
            there = []
            for zz in (j, j + 4):
                rows = buf[zz // 2, zz % 2 * 16 : zz % 2 * 16 + 16, cols].astype(jnp.float32)
                there.append(jnp.where(high, rows[8:], rows[:8]) + got[zz, :, cols])
            second = z_high(z, s, j)
            own[j * 8 : j * 8 + 8, cols] = jnp.where(second, there[1], there[0])
            out[j * 8 : j * 8 + 8, cols] = jnp.where(second, there[0], there[1])

    each_chunk(cut, body)


def call(kernel, outs, scratch, copies, local, *got):
    got = [pltpu.with_memory_space_constraint(v, pltpu.VMEM) for v in got]
    vmem = pl.BlockSpec(memory_space=pltpu.VMEM)
    return pl.pallas_call(
        kernel,
        in_specs=[pl.BlockSpec(memory_space=pl.ANY)] + [vmem] * len(got),
        out_specs=[vmem] * len(outs),
        out_shape=[pltpu.VMEM(shape, jnp.float32) for shape in outs],
        scratch_shapes=[pltpu.VMEM(shape, jnp.bfloat16) for shape in scratch] + [pltpu.SemaphoreType.DMA((copies,))],
        compiler_params=pltpu.CompilerParams(vmem_limit_bytes=4 << 20),
        cost_estimate=pl.CostEstimate(flops=1 << 18, bytes_accessed=1 << 20, transcendentals=0),
    )(local, *got)


def sum_parts(local):
    cols = local.shape[1]
    cut = cols * SHARE // TOTAL
    rest = cols - cut
    z, x, core, s = place()
    odd = lax.rem(x, 2) == 1

    (b_out,) = call(functools.partial(give_z_kernel, cut), [(4, 16, rest)], [(4, 16, rest)], 4, local)
    b_got = send_z_pair(b_out)
    later = lax.optimization_barrier((local, b_out))[0]
    (a_out,) = call(functools.partial(give_x_kernel, cut), [(NZ, 8, cut)], [(4, 32, cut)], 4, later)
    a_got = send_x_first(a_out)
    b_own, b_out = call(functools.partial(b_kernel, cut), [(32, rest)] * 2, [(4, 16, rest)], 4, local, b_got)
    b_got = send_x_first(b_out)
    later = lax.optimization_barrier((local, b_out))[0]
    a_own, a_out = call(functools.partial(a_kernel, cut), [(32, cut)] * 2, [(4, 32, cut)], 4, later, a_got)
    a_got = send_z_pair(a_out)
    own = jnp.concatenate([a_own + a_got, b_own + b_got], axis=1).reshape(4, 8, cols)
    own, out = jnp.where(odd, own[:, 4:], own[:, :4]), jnp.where(odd, own[:, :4], own[:, 4:])
    own = own + send_x_second(out)
    far = [send_z_far(pick(own, (z + s * k) & 3, 0), k) for k in ORDER]
    return pick(own, z & 3, 0) + far[0] + far[1] + far[2]


def sum_over_col(value):
    got = [lax.ppermute(value, "col", [(i, i ^ m) for i in range(NY)]) for m in COL_ORDER]
    return value + got[0] + got[1] + got[2]


def per_device(weight, momentum, grad_parts):
    gradient = sum_parts(grad_parts[0])
    squares = [jnp.sum(v * v, axis=1, keepdims=True) for v in (weight, gradient)]
    squares = sum_over_col(jnp.concatenate(squares, axis=1))
    weight_sq, grad_sq = squares[:, :1], squares[:, 1:]
    factor = jnp.minimum(1.0, clip_bound * jnp.sqrt(weight_sq) * lax.rsqrt(grad_sq + small_term))
    new_momentum = momentum_decay * momentum + factor * gradient
    return (weight - learn_rate * new_momentum, new_momentum)


def solution(mesh):
    in_specs = (P(("row", "dp"), "col"), P(("row", "dp"), "col"), P("dp", "row", "col"))
    out_specs = (P(("row", "dp"), "col"), P(("row", "dp"), "col"))
    return jax.shard_map(
        per_device, mesh=mesh, in_specs=in_specs, out_specs=out_specs, check_vma=False
    )
```

time: 63 us -> 57.1 us (0.906)
  starting transfers between devices: 26.1 us -> 23.3 us
  other arithmetic: 3.78 us -> 1.5 us
  local copies, waits for them, and re-layouts: 3.3 us -> 1.45 us
  Pallas kernels: 0 us -> 1.65 us
  waiting for transfers between devices: 28.6 us -> 27.9 us
    ppermute x9 -> x8, starting transfers between devices: 24 us -> 19.7 us  [send(): return lax.ppermute(value, ('dp', 'row'), pairs_zx(target))]
    ppermute x4 -> x3, waiting for transfers between devices: 7.33 us -> 3.5 us  [sum_over_col(): lax.ppermute(value, 'col', [(i, i ^ m) for i in range(NY)])]
    ppermute x9 -> x8, waiting for transfers between devices: 21.3 us -> 24.4 us  [send(): return lax.ppermute(value, ('dp', 'row'), pairs_zx(target))]
    add x8 -> x4, other arithmetic: 1.92 us -> 0.21 us  [the longest x1 0.12 us: sum_parts(): own = own + send_x_second(out)]
    pallas_call x0 -> x4, Pallas kernels: none -> 1.65 us  [call(): pl.pallas_call(kernel, in_specs=[pl.BlockSpec(memory_space=pl.ANY)] + [vm...]
    ppermute x4 -> x3, starting transfers between devices: 2.09 us -> 3.57 us  [sum_over_col(): lax.ppermute(value, 'col', [(i, i ^ m) for i in range(NY)])]
    slice x1 -> x0, local copies, waits for them, and re-layouts: 1.47 us -> none  [sum_parts(): a = local[:, :cut].reshape(NZ, NX, 4, cut)]
    unnamed x5 -> x6, local copies, waits for them, and re-layouts: 1 us -> 1.41 us
  transfers between devices with their start and end apart: 13 -> 11, of which waited for: 8 -> 10; matrix products, arithmetic and copies ran while one was open for 5% -> 0% of each run, Pallas kernels for 0% -> 2%
where the time goes in v2:
time: 57.1 us; the launch traced here: 56.5 us
  waiting for transfers between devices  27.9 us (49%)
  starting transfers between devices  23.3 us (41%)
  Pallas kernels  1.65 us (3%)
  other arithmetic  1.5 us (3%)
  local copies, waits for them, and re-layouts  1.45 us (3%)
  between operations  0.74 us (1%)
    ppermute x8, waiting for transfers between devices, send(): return lax.ppermute(value, ('dp', 'row'), pairs_zx(target))  24.4 us
    ppermute x8, starting transfers between devices, send(): return lax.ppermute(value, ('dp', 'row'), pairs_zx(target))  19.7 us
    ppermute x3, starting transfers between devices, sum_over_col(): lax.ppermute(value, 'col', [(i, i ^ m) for i in range(NY)])  3.57 us
    ppermute x3, waiting for transfers between devices, sum_over_col(): lax.ppermute(value, 'col', [(i, i ^ m) for i in range(NY)])  3.5 us
    pallas_call x4, Pallas kernels, call(): pl.pallas_call(kernel, in_specs=[pl.BlockSpec(memory_space=pl.ANY)] + [vm...  1.65 us
    unnamed x6, local copies, waits for them, and re-layouts  1.41 us
  transfers between devices with their start and end apart: 11, of which 10 were waited for; matrix products, arithmetic and copies ran while one was open for 0% of the time, Pallas kernels for 2%

profile of v2, /device:TPU:24, one launch (start us, length us, event | category | flops | bytes accessed | tf_op | source)
XLA Modules:
  0.0 56.5 jit_solution(3262577333322229146)
XLA Ops:
  0.6 0.0 copy-start
  0.6 1.4 %copy-done = bf16[1,128,6144]{2,1,0:T(8,128)(2,1)S(1)} copy-done((bf16[1,128,6144]{2,1,0:T(8,128)(2,1)S(1)}, bf16[1,128,6144]{2,1,0:T(8,128)(2,1)}, u32[]{:S(2)}) %copy-start) | copy-done | bytes 1572888
  2.0 0.4 shard_map.50
  2.4 2.0 %collective-permute-start = (f32[4,16,3072]{2,1,0:T(8,128)S(1)}, f32[4,16,3072]{2,1,0:T(8,128)S(1)}, u32[]{:S(2)}, u32[]{:S(2)}) collective-permute-start(f32[4,16,3072]{2,1,0:T(8,128)S(1)} %shard_map.50), channel_id=1, source_target_pairs={{0,32},{4,228},{8,40},{12,236},{16,48},{20,244},{24,56},{28,252},{... | collective-permute-start | bytes 2359304 | tf_op jit(solution)/shard_map/ppermute | solution.py:37
  4.4 0.4 shard_map.52
  4.8 1.6 %collective-permute-start.1 = (f32[8,8,3072]{2,1,0:T(8,128)S(1)}, f32[8,8,3072]{2,1,0:T(8,128)S(1)}, u32[]{:S(2)}, u32[]{:S(2)}) collective-permute-start(f32[8,8,3072]{2,1,0:T(8,128)S(1)} %shard_map.52), channel_id=1, source_target_pairs={{0,8},{4,28},{8,0},{12,20},{16,24},{20,12},{24,16},{28,4},{32,40},... | collective-permute-start | bytes 2359304 | tf_op jit(solution)/shard_map/ppermute | solution.py:37
  6.4 8.1 %collective-permute-done.got = f32[4,16,3072]{2,1,0:T(8,128)S(1)} collective-permute-done((f32[4,16,3072]{2,1,0:T(8,128)S(1)}, f32[4,16,3072]{2,1,0:T(8,128)S(1)}, u32[]{:S(2)}, u32[]{:S(2)}) %collective-permute-start) | collective-permute-done | bytes 786464 | tf_op jit(solution)/shard_map/ppermute | solution.py:37
  14.5 0.4 shard_map.51
  14.9 1.6 %collective-permute-start.3 = (f32[32,3072]{1,0:T(8,128)S(1)}, f32[32,3072]{1,0:T(8,128)S(1)}, u32[]{:S(2)}, u32[]{:S(2)}) collective-permute-start(f32[32,3072]{1,0:T(8,128)S(1)} %get-tuple-element.8), channel_id=1, source_target_pairs={{0,8},{4,28},{8,0},{12,20},{16,24},{20,12},{24,16},{28,4},{32,40},... | collective-permute-start | bytes 1179656 | tf_op jit(solution)/shard_map/ppermute | solution.py:37
  16.5 0.4 collective-permute-done.1.got
  16.9 0.5 shard_map.53
  17.4 1.6 %collective-permute-start.2 = (f32[32,3072]{1,0:T(8,128)S(1)}, f32[32,3072]{1,0:T(8,128)S(1)}, u32[]{:S(2)}, u32[]{:S(2)}) collective-permute-start(f32[32,3072]{1,0:T(8,128)S(1)} %get-tuple-element.12), channel_id=1, source_target_pairs={{0,32},{4,228},{8,40},{12,236},{16,48},{20,244},{24,56},{28,252},{... | collective-permute-start | bytes 1179656 | tf_op jit(solution)/shard_map/ppermute | solution.py:37
  19.0 3.8 %collective-permute-done.3 = f32[32,3072]{1,0:T(8,128)S(1)} collective-permute-done((f32[32,3072]{1,0:T(8,128)S(1)}, f32[32,3072]{1,0:T(8,128)S(1)}, u32[]{:S(2)}, u32[]{:S(2)}) %collective-permute-start.3) | collective-permute-done | bytes 393248 | tf_op jit(solution)/shard_map/ppermute | solution.py:37
  22.8 2.4 %collective-permute-done.2 = f32[32,3072]{1,0:T(8,128)S(1)} collective-permute-done((f32[32,3072]{1,0:T(8,128)S(1)}, f32[32,3072]{1,0:T(8,128)S(1)}, u32[]{:S(2)}, u32[]{:S(2)}) %collective-permute-start.2) | collective-permute-done | bytes 393248 | tf_op jit(solution)/shard_map/ppermute | solution.py:37
  25.3 0.1 maximum_bitcast_fusion
  25.3 0.0 copy-start.1
  25.4 0.1 slice_select_fusion
  25.5 0.0 copy-start.2
  25.5 2.8 %collective-permute-start.4 = (f32[4,4,6144]{2,1,0:T(4,128)S(1)}, f32[4,4,6144]{2,1,0:T(4,128)S(1)}, u32[]{:S(2)}, u32[]{:S(2)}) collective-permute-start(f32[4,4,6144]{2,1,0:T(4,128)S(1)} %slice_select_fusion), channel_id=1, source_target_pairs={{0,24},{4,12},{8,16},{12,4},{16,8},{20,28},{24,0},{28,20},{32,56},... | collective-permute-start | bytes 1179656 | tf_op jit(solution)/shard_map/ppermute | solution.py:37
  28.3 6.2 %collective-permute-done.4 = f32[4,4,6144]{2,1,0:T(4,128)S(1)} collective-permute-done((f32[4,4,6144]{2,1,0:T(4,128)S(1)}, f32[4,4,6144]{2,1,0:T(4,128)S(1)}, u32[]{:S(2)}, u32[]{:S(2)}) %collective-permute-start.4) | collective-permute-done | bytes 393248 | tf_op jit(solution)/shard_map/ppermute | solution.py:37
  34.5 0.1 select_add_fusion
  34.7 6.4 %collective-permute-start.7 = (f32[4,6144]{1,0:T(4,128)S(1)}, f32[4,6144]{1,0:T(4,128)S(1)}, u32[]{:S(2)}, u32[]{:S(2)}) collective-permute-start(f32[4,6144]{1,0:T(4,128)S(1)} %get-tuple-element.19), channel_id=1, source_target_pairs={{0,160},{4,100},{8,168},{12,108},{16,176},{20,116},{24,184},{28,12... | collective-permute-start | bytes 294920 | tf_op jit(solution)/shard_map/ppermute | solution.py:37
  41.1 0.6 collective-permute-start.6
  41.7 3.1 %collective-permute-start.5 = (f32[4,6144]{1,0:T(4,128)S(1)}, f32[4,6144]{1,0:T(4,128)S(1)}, u32[]{:S(2)}, u32[]{:S(2)}) collective-permute-start(f32[4,6144]{1,0:T(4,128)S(1)} %get-tuple-element.18), channel_id=1, source_target_pairs={{0,224},{4,36},{8,232},{12,44},{16,240},{20,52},{24,248},{28,60},{... | collective-permute-start | bytes 294920 | tf_op jit(solution)/shard_map/ppermute | solution.py:37
  44.8 0.0 copy-done.1
  44.8 0.2 multiply_reduce_fusion.1
  45.0 0.0 collective-permute-done.7
  45.0 1.8 %collective-permute-done.6 = f32[4,6144]{1,0:T(4,128)S(1)} collective-permute-done((f32[4,6144]{1,0:T(4,128)S(1)}, f32[4,6144]{1,0:T(4,128)S(1)}, u32[]{:S(2)}, u32[]{:S(2)}) %collective-permute-start.6) | collective-permute-done | bytes 98336 | tf_op jit(solution)/shard_map/ppermute | solution.py:37
  46.8 1.7 %collective-permute-done.5 = f32[4,6144]{1,0:T(4,128)S(1)} collective-permute-done((f32[4,6144]{1,0:T(4,128)S(1)}, f32[4,6144]{1,0:T(4,128)S(1)}, u32[]{:S(2)}, u32[]{:S(2)}) %collective-permute-start.5) | collective-permute-done | bytes 98336 | tf_op jit(solution)/shard_map/ppermute | solution.py:37
  48.5 0.2 multiply_reduce_fusion
  48.7 1.3 %collective-permute-start.10 = (f32[4,2]{0,1:T(2,128)S(1)}, f32[4,2]{0,1:T(2,128)S(1)}, u32[]{:S(2)}, u32[]{:S(2)}) collective-permute-start(f32[4,2]{0,1:T(2,128)S(1)} %pad_maximum_fusion), channel_id=1, source_target_pairs={{0,2},{1,3},{2,0},{3,1},{4,6},{5,7},{6,4},{7,5},{8,10},{9,11},{10,... | collective-permute-start | bytes 104 | tf_op jit(solution)/shard_map/ppermute | solution.py:204
  50.0 2.2 %collective-permute-start.9 = (f32[4,2]{0,1:T(2,128)S(1)}, f32[4,2]{0,1:T(2,128)S(1)}, u32[]{:S(2)}, u32[]{:S(2)}) collective-permute-start(f32[4,2]{0,1:T(2,128)S(1)} %pad_maximum_fusion), channel_id=1, source_target_pairs={{0,3},{1,2},{2,1},{3,0},{4,7},{5,6},{6,5},{7,4},{8,11},{9,10},{10,... | collective-permute-start | bytes 104 | tf_op jit(solution)/shard_map/ppermute | solution.py:204
  52.2 0.1 collective-permute-start.8
  52.2 1.6 %collective-permute-done.10 = f32[4,2]{0,1:T(2,128)S(1)} collective-permute-done((f32[4,2]{0,1:T(2,128)S(1)}, f32[4,2]{0,1:T(2,128)S(1)}, u32[]{:S(2)}, u32[]{:S(2)}) %collective-permute-start.10) | collective-permute-done | bytes 64 | tf_op jit(solution)/shard_map/ppermute | solution.py:204
  53.8 0.9 %collective-permute-done.9 = f32[4,2]{0,1:T(2,128)S(1)} collective-permute-done((f32[4,2]{0,1:T(2,128)S(1)}, f32[4,2]{0,1:T(2,128)S(1)}, u32[]{:S(2)}, u32[]{:S(2)}) %collective-permute-start.9) | collective-permute-done | bytes 64 | tf_op jit(solution)/shard_map/ppermute | solution.py:204
  54.8 1.0 %collective-permute-done.8 = f32[4,2]{0,1:T(2,128)S(1)} collective-permute-done((f32[4,2]{0,1:T(2,128)S(1)}, f32[4,2]{0,1:T(2,128)S(1)}, u32[]{:S(2)}, u32[]{:S(2)}) %collective-permute-start.8) | collective-permute-done | bytes 64 | tf_op jit(solution)/shard_map/ppermute | solution.py:204
  55.8 0.0 copy-done.2
  55.8 0.8 %fusion.2 = (f32[4,6144]{1,0:T(4,128)}, f32[4,6144]{1,0:T(4,128)}) fusion(f32[4,6144]{1,0:T(4,128)S(1)} %copy-done.1, f32[4,6144]{1,0:T(4,128)S(1)} %get-tuple-element.17, f32[4]{0:T(128)S(1)} %minimum_bitcast_fusion, f32[4,6144]{1,0:T(4,128)S(1)} %copy-done.2), kind=kLoop, calls=%fused_computation.15 | loop fusion | flops 98304 | bytes 491536 | tf_op jit(solution)/shard_map/sub | solution.py:215
  (6 shorter events, 0.1 us)
Async XLA Ops:
  0.6 1.4 %copy-start = (bf16[1,128,6144]{2,1,0:T(8,128)(2,1)S(1)}, bf16[1,128,6144]{2,1,0:T(8,128)(2,1)}, u32[]{:S(2)}) copy-start(bf16[1,128,6144]{2,1,0:T(8,128)(2,1)} %param.5) | copy-start | bytes 4718596
  2.4 12.1 %collective-permute-start = (f32[4,16,3072]{2,1,0:T(8,128)S(1)}, f32[4,16,3072]{2,1,0:T(8,128)S(1)}, u32[]{:S(2)}, u32[]{:S(2)}) collective-permute-start(f32[4,16,3072]{2,1,0:T(8,128)S(1)} %shard_map.50), channel_id=1, source_target_pairs={{0,32},{4,228},{8,40},{12,236},{16,48},{20,244},{24,56},{28,252},{... | collective-permute-start | bytes 2359304 | tf_op jit(solution)/shard_map/ppermute | solution.py:37
  4.8 12.1 %collective-permute-start.1 = (f32[8,8,3072]{2,1,0:T(8,128)S(1)}, f32[8,8,3072]{2,1,0:T(8,128)S(1)}, u32[]{:S(2)}, u32[]{:S(2)}) collective-permute-start(f32[8,8,3072]{2,1,0:T(8,128)S(1)} %shard_map.52), channel_id=1, source_target_pairs={{0,8},{4,28},{8,0},{12,20},{16,24},{20,12},{24,16},{28,4},{32,40},... | collective-permute-start | bytes 2359304 | tf_op jit(solution)/shard_map/ppermute | solution.py:37
  14.9 7.9 %collective-permute-start.3 = (f32[32,3072]{1,0:T(8,128)S(1)}, f32[32,3072]{1,0:T(8,128)S(1)}, u32[]{:S(2)}, u32[]{:S(2)}) collective-permute-start(f32[32,3072]{1,0:T(8,128)S(1)} %get-tuple-element.8), channel_id=1, source_target_pairs={{0,8},{4,28},{8,0},{12,20},{16,24},{20,12},{24,16},{28,4},{32,40},... | collective-permute-start | bytes 1179656 | tf_op jit(solution)/shard_map/ppermute | solution.py:37
  17.4 7.9 %collective-permute-start.2 = (f32[32,3072]{1,0:T(8,128)S(1)}, f32[32,3072]{1,0:T(8,128)S(1)}, u32[]{:S(2)}, u32[]{:S(2)}) collective-permute-start(f32[32,3072]{1,0:T(8,128)S(1)} %get-tuple-element.12), channel_id=1, source_target_pairs={{0,32},{4,228},{8,40},{12,236},{16,48},{20,244},{24,56},{28,252},{... | collective-permute-start | bytes 1179656 | tf_op jit(solution)/shard_map/ppermute | solution.py:37
  25.3 19.5 %copy-start.1 = (f32[4,6144]{1,0:T(4,128)S(1)}, f32[4,6144]{1,0:T(4,128)}, u32[]{:S(2)}) copy-start(f32[4,6144]{1,0:T(4,128)} %param.3) | copy-start | bytes 294916
  25.5 30.3 %copy-start.2 = (f32[4,6144]{1,0:T(4,128)S(1)}, f32[4,6144]{1,0:T(4,128)}, u32[]{:S(2)}) copy-start(f32[4,6144]{1,0:T(4,128)} %param.4) | copy-start | bytes 294916
  25.5 9.1 %collective-permute-start.4 = (f32[4,4,6144]{2,1,0:T(4,128)S(1)}, f32[4,4,6144]{2,1,0:T(4,128)S(1)}, u32[]{:S(2)}, u32[]{:S(2)}) collective-permute-start(f32[4,4,6144]{2,1,0:T(4,128)S(1)} %slice_select_fusion), channel_id=1, source_target_pairs={{0,24},{4,12},{8,16},{12,4},{16,8},{20,28},{24,0},{28,20},{32,56},... | collective-permute-start | bytes 1179656 | tf_op jit(solution)/shard_map/ppermute | solution.py:37
  34.7 10.3 %collective-permute-start.7 = (f32[4,6144]{1,0:T(4,128)S(1)}, f32[4,6144]{1,0:T(4,128)S(1)}, u32[]{:S(2)}, u32[]{:S(2)}) collective-permute-start(f32[4,6144]{1,0:T(4,128)S(1)} %get-tuple-element.19), channel_id=1, source_target_pairs={{0,160},{4,100},{8,168},{12,108},{16,176},{20,116},{24,184},{28,12... | collective-permute-start | bytes 294920 | tf_op jit(solution)/shard_map/ppermute | solution.py:37
  41.1 5.6 %collective-permute-start.6 = (f32[4,6144]{1,0:T(4,128)S(1)}, f32[4,6144]{1,0:T(4,128)S(1)}, u32[]{:S(2)}, u32[]{:S(2)}) collective-permute-start(f32[4,6144]{1,0:T(4,128)S(1)} %get-tuple-element.20), channel_id=1, source_target_pairs={{0,192},{4,68},{8,200},{12,76},{16,208},{20,84},{24,216},{28,92},{... | collective-permute-start | bytes 294920 | tf_op jit(solution)/shard_map/ppermute | solution.py:37
  41.7 6.8 %collective-permute-start.5 = (f32[4,6144]{1,0:T(4,128)S(1)}, f32[4,6144]{1,0:T(4,128)S(1)}, u32[]{:S(2)}, u32[]{:S(2)}) collective-permute-start(f32[4,6144]{1,0:T(4,128)S(1)} %get-tuple-element.18), channel_id=1, source_target_pairs={{0,224},{4,36},{8,232},{12,44},{16,240},{20,52},{24,248},{28,60},{... | collective-permute-start | bytes 294920 | tf_op jit(solution)/shard_map/ppermute | solution.py:37
  48.7 5.2 %collective-permute-start.10 = (f32[4,2]{0,1:T(2,128)S(1)}, f32[4,2]{0,1:T(2,128)S(1)}, u32[]{:S(2)}, u32[]{:S(2)}) collective-permute-start(f32[4,2]{0,1:T(2,128)S(1)} %pad_maximum_fusion), channel_id=1, source_target_pairs={{0,2},{1,3},{2,0},{3,1},{4,6},{5,7},{6,4},{7,5},{8,10},{9,11},{10,... | collective-permute-start | bytes 104 | tf_op jit(solution)/shard_map/ppermute | solution.py:204
  50.0 4.8 %collective-permute-start.9 = (f32[4,2]{0,1:T(2,128)S(1)}, f32[4,2]{0,1:T(2,128)S(1)}, u32[]{:S(2)}, u32[]{:S(2)}) collective-permute-start(f32[4,2]{0,1:T(2,128)S(1)} %pad_maximum_fusion), channel_id=1, source_target_pairs={{0,3},{1,2},{2,1},{3,0},{4,7},{5,6},{6,5},{7,4},{8,11},{9,10},{10,... | collective-permute-start | bytes 104 | tf_op jit(solution)/shard_map/ppermute | solution.py:204
  52.2 3.6 %collective-permute-start.8 = (f32[4,2]{0,1:T(2,128)S(1)}, f32[4,2]{0,1:T(2,128)S(1)}, u32[]{:S(2)}, u32[]{:S(2)}) collective-permute-start(f32[4,2]{0,1:T(2,128)S(1)} %pad_maximum_fusion), channel_id=1, source_target_pairs={{0,1},{1,0},{2,3},{3,2},{4,5},{5,4},{6,7},{7,6},{8,9},{9,8},{10,11... | collective-permute-start | bytes 104 | tf_op jit(solution)/shard_map/ppermute | solution.py:204

commit v3 on v2

--- a/solution.py
+++ b/solution.py
@@ -13,9 +13,10 @@
 learn_rate = 1.0
 
 NZ, NX, NY, NCORE = 8, 4, 4, 2
-SHARE, TOTAL = 1, 2
+PIECES = 3
+LIMIT = 2 << 20
 CHUNK = 512
-ORDER = (1, 2, 3)
+ORDER = (3, 2, 1)
 COL_ORDER = (1, 3, 2)
 
 
@@ -57,6 +58,10 @@
     return lax.dynamic_index_in_dim(value, index, axis, keepdims=False)
 
 
+def after(value, other):
+    return lax.optimization_barrier((value, other))[0]
+
+
 def place():
     dp, core = lax.axis_index("dp"), lax.axis_index("row")
     z, x = lax.div(dp, NX), lax.rem(dp, NX)
@@ -77,12 +82,12 @@
     lax.fori_loop(0, cols // n, lambda i, c: (body(pl.multiple_of(i * n, n), n), c)[1], 0)
 
 
-def give_z_kernel(cut, src, out, buf, sem):
+def give_z_kernel(start, src, out, buf, sem):
     z, x, core, s = place()
     copies = []
     for j in range(4):
         row = pl.multiple_of(jnp.where(z_high(z, s, j), 0, 64) + j * 16, 16)
-        copies.append(pltpu.make_async_copy(src.at[pl.ds(row, 16), pl.ds(cut, buf.shape[2])], buf.at[j], sem.at[j]))
+        copies.append(pltpu.make_async_copy(src.at[pl.ds(row, 16), pl.ds(start, buf.shape[2])], buf.at[j], sem.at[j]))
     for copy in copies:
         copy.start()
     for copy in copies:
@@ -96,10 +101,10 @@
     each_chunk(buf.shape[2], body)
 
 
-def give_x_kernel(cut, src, out, buf, sem):
+def give_x_kernel(start, src, out, buf, sem):
     z, x, core, s = place()
     copies = [
-        pltpu.make_async_copy(src.at[pl.ds(j * 32, 32), pl.ds(0, cut)], buf.at[j], sem.at[j]) for j in range(4)
+        pltpu.make_async_copy(src.at[pl.ds(j * 32, 32), pl.ds(start, buf.shape[2])], buf.at[j], sem.at[j]) for j in range(4)
     ]
     for copy in copies:
         copy.start()
@@ -112,15 +117,15 @@
             rows = buf[k // 2, k % 2 * 16 : k % 2 * 16 + 16, pl.ds(first, n)].astype(jnp.float32)
             out[k, :, pl.ds(first, n)] = jnp.where(high, rows[8:], rows[:8])
 
-    each_chunk(cut, body)
-
-
-def b_kernel(cut, src, got, own, out, buf, sem):
+    each_chunk(buf.shape[2], body)
+
+
+def b_kernel(start, src, got, own, out, buf, sem):
     z, x, core, s = place()
     copies = []
     for j in range(4):
         row = pl.multiple_of(jnp.where(z_high(z, s, j), 64, 0) + j * 16, 16)
-        copies.append(pltpu.make_async_copy(src.at[pl.ds(row, 16), pl.ds(cut, buf.shape[2])], buf.at[j], sem.at[j]))
+        copies.append(pltpu.make_async_copy(src.at[pl.ds(row, 16), pl.ds(start, buf.shape[2])], buf.at[j], sem.at[j]))
     for copy in copies:
         copy.start()
     for copy in copies:
@@ -137,10 +142,10 @@
     each_chunk(buf.shape[2], body)
 
 
-def a_kernel(cut, src, got, own, out, buf, sem):
+def a_kernel(start, src, got, own, out, buf, sem):
     z, x, core, s = place()
     copies = [
-        pltpu.make_async_copy(src.at[pl.ds(j * 32, 32), pl.ds(0, cut)], buf.at[j], sem.at[j]) for j in range(4)
+        pltpu.make_async_copy(src.at[pl.ds(j * 32, 32), pl.ds(start, buf.shape[2])], buf.at[j], sem.at[j]) for j in range(4)
     ]
     for copy in copies:
         copy.start()
@@ -159,45 +164,91 @@
             own[j * 8 : j * 8 + 8, cols] = jnp.where(second, there[1], there[0])
             out[j * 8 : j * 8 + 8, cols] = jnp.where(second, there[0], there[1])
 
-    each_chunk(cut, body)
-
-
-def call(kernel, outs, scratch, copies, local, *got):
-    got = [pltpu.with_memory_space_constraint(v, pltpu.VMEM) for v in got]
+    each_chunk(buf.shape[2], body)
+
+
+def join_kernel(a, a_got, b, b_got, own, out):
+    z, x, core, s = place()
+    odd = lax.rem(x, 2) == 1
+
+    def body(first, n):
+        top = lax.broadcasted_iota(jnp.int32, (8, n), 0) < 4
+        for kept, got, start in ((b, b_got, a.shape[1]), (a, a_got, 0)):
+            for j in range(2):
+                there = []
+                for i in range(2):
+                    here = (slice((2 * j + i) * 8, (2 * j + i) * 8 + 8), pl.ds(first, n))
+                    rows = kept[here] + got[here]
+                    turned = jnp.concatenate([rows[4:], rows[:4]], axis=0)
+                    there.append((jnp.where(odd, turned, rows), jnp.where(odd, rows, turned)))
+                here = (slice(j * 8, j * 8 + 8), pl.ds(start + first, n))
+                own[here] = jnp.where(top, there[0][0], there[1][1])
+                out[here] = jnp.where(top, there[0][1], there[1][0])
+
+    each_chunk(a.shape[1], body)
+
+
+def call(kernel, outs, scratch, *args):
     vmem = pl.BlockSpec(memory_space=pltpu.VMEM)
+    specs = [vmem] * len(args)
+    if scratch:
+        specs[0] = pl.BlockSpec(memory_space=pl.ANY)
+    args = [v if spec is not vmem else pltpu.with_memory_space_constraint(v, pltpu.VMEM) for v, spec in zip(args, specs)]
     return pl.pallas_call(
         kernel,
-        in_specs=[pl.BlockSpec(memory_space=pl.ANY)] + [vmem] * len(got),
+        in_specs=specs,
         out_specs=[vmem] * len(outs),
         out_shape=[pltpu.VMEM(shape, jnp.float32) for shape in outs],
-        scratch_shapes=[pltpu.VMEM(shape, jnp.bfloat16) for shape in scratch] + [pltpu.SemaphoreType.DMA((copies,))],
-        compiler_params=pltpu.CompilerParams(vmem_limit_bytes=4 << 20),
-        cost_estimate=pl.CostEstimate(flops=1 << 18, bytes_accessed=1 << 20, transcendentals=0),
-    )(local, *got)
+        scratch_shapes=[pltpu.VMEM(scratch, jnp.bfloat16), pltpu.SemaphoreType.DMA((scratch[0],))] if scratch else [],
+        compiler_params=pltpu.CompilerParams(vmem_limit_bytes=LIMIT),
+        cost_estimate=pl.CostEstimate(flops=1024, bytes_accessed=1024, transcendentals=0),
+    )(*args)
+
+
+def last_step(own, z, s):
+    out, last = [], None
+    for k in ORDER:
+        part = pick(own, (z + s * k) & 3, 0)
+        out.append(part if last is None else after(part, last))
+        last = out[-1]
+    total = pick(own, z & 3, 0)
+    for part, k in zip(out, ORDER):
+        total = total + send_z_far(part, k)
+    return total
 
 
 def sum_parts(local):
     cols = local.shape[1]
-    cut = cols * SHARE // TOTAL
-    rest = cols - cut
+    n = cols // (2 * PIECES)
+    a_at, b_at = [2 * i * n for i in range(PIECES)], [(2 * i + 1) * n for i in range(PIECES)]
     z, x, core, s = place()
     odd = lax.rem(x, 2) == 1
 
-    (b_out,) = call(functools.partial(give_z_kernel, cut), [(4, 16, rest)], [(4, 16, rest)], 4, local)
-    b_got = send_z_pair(b_out)
-    later = lax.optimization_barrier((local, b_out))[0]
-    (a_out,) = call(functools.partial(give_x_kernel, cut), [(NZ, 8, cut)], [(4, 32, cut)], 4, later)
-    a_got = send_x_first(a_out)
-    b_own, b_out = call(functools.partial(b_kernel, cut), [(32, rest)] * 2, [(4, 16, rest)], 4, local, b_got)
-    b_got = send_x_first(b_out)
-    later = lax.optimization_barrier((local, b_out))[0]
-    a_own, a_out = call(functools.partial(a_kernel, cut), [(32, cut)] * 2, [(4, 32, cut)], 4, later, a_got)
-    a_got = send_z_pair(a_out)
-    own = jnp.concatenate([a_own + a_got, b_own + b_got], axis=1).reshape(4, 8, cols)
-    own, out = jnp.where(odd, own[:, 4:], own[:, :4]), jnp.where(odd, own[:, :4], own[:, 4:])
-    own = own + send_x_second(out)
-    far = [send_z_far(pick(own, (z + s * k) & 3, 0), k) for k in ORDER]
-    return pick(own, z & 3, 0) + far[0] + far[1] + far[2]
+    later, a_got, b_got = local, [], []
+    for a, b in zip(a_at, b_at):
+        (out,) = call(functools.partial(give_z_kernel, b), [(4, 16, n)], (4, 16, n), later)
+        b_got.append(send_z_pair(out))
+        later = after(local, out)
+        (out,) = call(functools.partial(give_x_kernel, a), [(NZ, 8, n)], (4, 32, n), later)
+        a_got.append(send_x_first(out))
+        later = after(local, out)
+    a_own, b_own = [], []
+    for i in range(PIECES):
+        own, out = call(functools.partial(b_kernel, b_at[i]), [(32, n)] * 2, (4, 16, n), later, b_got[i])
+        b_own.append((own, send_x_first(out)))
+        later = after(local, out)
+        own, out = call(functools.partial(a_kernel, a_at[i]), [(32, n)] * 2, (4, 32, n), later, a_got[i])
+        a_own.append((own, send_z_pair(out)))
+        later = after(local, out)
+    kept, last = [], None
+    for (a, a_got), (b, b_got) in zip(a_own, b_own):
+        own, out = call(join_kernel, [(16, 2 * n)] * 2, None, a if last is None else after(a, last), a_got, b, b_got)
+        kept.append((own, send_x_second(out)))
+        last = out
+    done = []
+    for own, got in kept:
+        done.append((after(own, done[-1]) if done else own) + got)
+    return last_step(jnp.concatenate(done, axis=1).reshape(4, 4, cols), z, s)
 
 
 def sum_over_col(value):

time: 57.1 us -> 53 us (0.928)
  waiting for transfers between devices: 27.9 us -> 14.2 us
  starting transfers between devices: 23.3 us -> 32 us
    ppermute x8 -> x18, waiting for transfers between devices: 24.4 us -> 10.7 us  [send(): return lax.ppermute(value, ('dp', 'row'), pairs_zx(target))]
    ppermute x8 -> x18, starting transfers between devices: 19.7 us -> 28.5 us  [send(): return lax.ppermute(value, ('dp', 'row'), pairs_zx(target))]
    pallas_call x4 -> x15, Pallas kernels: 1.65 us -> 2.07 us  [call(): pl.pallas_call(kernel, in_specs=specs, out_specs=[vmem] * len(outs), out_...]
  transfers between devices with their start and end apart: 11 -> 21, of which waited for: 10 -> 10; matrix products, arithmetic and copies ran while one was open for 0% -> 0% of each run, Pallas kernels for 2% -> 4%
where the time goes in v3:
time: 53 us; the launch traced here: 52 us
  starting transfers between devices  32 us (60%)
  waiting for transfers between devices  14.2 us (27%)
  Pallas kernels  2.07 us (4%)
  local copies, waits for them, and re-layouts  1.56 us (3%)
  other arithmetic  1.23 us (2%)
  between operations  0.85 us (2%)
    ppermute x18, starting transfers between devices, send(): return lax.ppermute(value, ('dp', 'row'), pairs_zx(target))  28.5 us
    ppermute x18, waiting for transfers between devices, send(): return lax.ppermute(value, ('dp', 'row'), pairs_zx(target))  10.7 us
    ppermute x3, starting transfers between devices, sum_over_col(): lax.ppermute(value, 'col', [(i, i ^ m) for i in range(NY)])  3.57 us
    ppermute x3, waiting for transfers between devices, sum_over_col(): lax.ppermute(value, 'col', [(i, i ^ m) for i in range(NY)])  3.5 us
    pallas_call x15, Pallas kernels, call(): pl.pallas_call(kernel, in_specs=specs, out_specs=[vmem] * len(outs), out_...  2.07 us
    unnamed x6, local copies, waits for them, and re-layouts  1.41 us
  transfers between devices with their start and end apart: 21, of which 10 were waited for; matrix products, arithmetic and copies ran while one was open for 0% of the time, Pallas kernels for 4%

profile of v3, /device:TPU:24, one launch (start us, length us, event | category | flops | bytes accessed | tf_op | source)
XLA Modules:
  0.0 52.0 jit_solution(7670916488403354030)
XLA Ops:
  0.6 1.4 %copy-done = bf16[1,128,6144]{2,1,0:T(8,128)(2,1)S(1)} copy-done((bf16[1,128,6144]{2,1,0:T(8,128)(2,1)S(1)}, bf16[1,128,6144]{2,1,0:T(8,128)(2,1)}, u32[]{:S(2)}) %copy-start) | copy-done | bytes 1572888
  2.0 0.1 shard_map.50
  2.2 2.0 %collective-permute-start = (f32[4,16,1024]{2,1,0:T(8,128)S(1)}, f32[4,16,1024]{2,1,0:T(8,128)S(1)}, u32[]{:S(2)}, u32[]{:S(2)}) collective-permute-start(f32[4,16,1024]{2,1,0:T(8,128)S(1)} %shard_map.50), channel_id=1, source_target_pairs={{0,32},{4,228},{8,40},{12,236},{16,48},{20,244},{24,56},{28,252},{... | collective-permute-start | bytes 786440 | tf_op jit(solution)/shard_map/ppermute | solution.py:38
  4.2 0.2 shard_map.51
  4.3 1.6 %collective-permute-start.1 = (f32[8,8,1024]{2,1,0:T(8,128)S(1)}, f32[8,8,1024]{2,1,0:T(8,128)S(1)}, u32[]{:S(2)}, u32[]{:S(2)}) collective-permute-start(f32[8,8,1024]{2,1,0:T(8,128)S(1)} %shard_map.51), channel_id=1, source_target_pairs={{0,8},{4,28},{8,0},{12,20},{16,24},{20,12},{24,16},{28,4},{32,40},... | collective-permute-start | bytes 786440 | tf_op jit(solution)/shard_map/ppermute | solution.py:38
  5.9 0.1 shard_map.52
  6.1 0.2 collective-permute-start.5
  6.3 0.2 shard_map.53
  6.4 0.6 %collective-permute-start.6 = (f32[8,8,1024]{2,1,0:T(8,128)S(1)}, f32[8,8,1024]{2,1,0:T(8,128)S(1)}, u32[]{:S(2)}, u32[]{:S(2)}) collective-permute-start(f32[8,8,1024]{2,1,0:T(8,128)S(1)} %shard_map.53), channel_id=1, source_target_pairs={{0,8},{4,28},{8,0},{12,20},{16,24},{20,12},{24,16},{28,4},{32,40},... | collective-permute-start | bytes 786440 | tf_op jit(solution)/shard_map/ppermute | solution.py:38
  7.1 0.1 shard_map.54
  7.2 2.0 %collective-permute-start.10 = (f32[4,16,1024]{2,1,0:T(8,128)S(1)}, f32[4,16,1024]{2,1,0:T(8,128)S(1)}, u32[]{:S(2)}, u32[]{:S(2)}) collective-permute-start(f32[4,16,1024]{2,1,0:T(8,128)S(1)} %shard_map.54), channel_id=1, source_target_pairs={{0,32},{4,228},{8,40},{12,236},{16,48},{20,244},{24,56},{28,252},{... | collective-permute-start | bytes 786440 | tf_op jit(solution)/shard_map/ppermute | solution.py:38
  9.2 0.2 shard_map.55
  9.4 0.0 collective-permute-done.got
  9.4 1.6 %collective-permute-start.11 = (f32[8,8,1024]{2,1,0:T(8,128)S(1)}, f32[8,8,1024]{2,1,0:T(8,128)S(1)}, u32[]{:S(2)}, u32[]{:S(2)}) collective-permute-start(f32[8,8,1024]{2,1,0:T(8,128)S(1)} %shard_map.55), channel_id=1, source_target_pairs={{0,8},{4,28},{8,0},{12,20},{16,24},{20,12},{24,16},{28,4},{32,40},... | collective-permute-start | bytes 786440 | tf_op jit(solution)/shard_map/ppermute | solution.py:38
  11.0 0.2 shard_map.56
  11.1 0.0 collective-permute-done.1.got
  11.1 0.2 shard_map.57
  11.3 1.2 %collective-permute-start.2 = (f32[32,1024]{1,0:T(8,128)S(1)}, f32[32,1024]{1,0:T(8,128)S(1)}, u32[]{:S(2)}, u32[]{:S(2)}) collective-permute-start(f32[32,1024]{1,0:T(8,128)S(1)} %get-tuple-element.46), channel_id=1, source_target_pairs={{0,32},{4,228},{8,40},{12,236},{16,48},{20,244},{24,56},{28,252},{... | collective-permute-start | bytes 393224 | tf_op jit(solution)/shard_map/ppermute | solution.py:38
  12.5 0.0 collective-permute-done.5.got
  12.5 0.5 %collective-permute-start.3 = (f32[32,1024]{1,0:T(8,128)S(1)}, f32[32,1024]{1,0:T(8,128)S(1)}, u32[]{:S(2)}, u32[]{:S(2)}) collective-permute-start(f32[32,1024]{1,0:T(8,128)S(1)} %get-tuple-element.43), channel_id=1, source_target_pairs={{0,8},{4,28},{8,0},{12,20},{16,24},{20,12},{24,16},{28,4},{32,40},... | collective-permute-start | bytes 393224 | tf_op jit(solution)/shard_map/ppermute | solution.py:38
  13.1 0.2 shard_map.59
  13.2 0.4 collective-permute-done.6.got
  13.6 0.2 shard_map.60
  13.8 1.5 %collective-permute-start.7 = (f32[32,1024]{1,0:T(8,128)S(1)}, f32[32,1024]{1,0:T(8,128)S(1)}, u32[]{:S(2)}, u32[]{:S(2)}) collective-permute-start(f32[32,1024]{1,0:T(8,128)S(1)} %get-tuple-element.55), channel_id=1, source_target_pairs={{0,32},{4,228},{8,40},{12,236},{16,48},{20,244},{24,56},{28,252},{... | collective-permute-start | bytes 393224 | tf_op jit(solution)/shard_map/ppermute | solution.py:38
  15.3 0.0 collective-permute-done.10.got
  15.3 0.6 %collective-permute-start.8 = (f32[32,1024]{1,0:T(8,128)S(1)}, f32[32,1024]{1,0:T(8,128)S(1)}, u32[]{:S(2)}, u32[]{:S(2)}) collective-permute-start(f32[32,1024]{1,0:T(8,128)S(1)} %get-tuple-element.51), channel_id=1, source_target_pairs={{0,8},{4,28},{8,0},{12,20},{16,24},{20,12},{24,16},{28,4},{32,40},... | collective-permute-start | bytes 393224 | tf_op jit(solution)/shard_map/ppermute | solution.py:38
  16.0 0.2 shard_map.62
  16.1 0.3 collective-permute-done.11.got
  16.4 0.2 shard_map.63
  16.6 1.5 %collective-permute-start.12 = (f32[32,1024]{1,0:T(8,128)S(1)}, f32[32,1024]{1,0:T(8,128)S(1)}, u32[]{:S(2)}, u32[]{:S(2)}) collective-permute-start(f32[32,1024]{1,0:T(8,128)S(1)} %get-tuple-element.65), channel_id=1, source_target_pairs={{0,32},{4,228},{8,40},{12,236},{16,48},{20,244},{24,56},{28,252},{... | collective-permute-start | bytes 393224 | tf_op jit(solution)/shard_map/ppermute | solution.py:38
  18.1 0.0 collective-permute-done.2.a_got
  18.1 0.6 %collective-permute-start.13 = (f32[32,1024]{1,0:T(8,128)S(1)}, f32[32,1024]{1,0:T(8,128)S(1)}, u32[]{:S(2)}, u32[]{:S(2)}) collective-permute-start(f32[32,1024]{1,0:T(8,128)S(1)} %get-tuple-element.61), channel_id=1, source_target_pairs={{0,8},{4,28},{8,0},{12,20},{16,24},{20,12},{24,16},{28,4},{32,40},... | collective-permute-start | bytes 393224 | tf_op jit(solution)/shard_map/ppermute | solution.py:38
  18.7 0.0 collective-permute-done.3.b_got
  18.7 0.1 shard_map.58
  18.8 2.8 %collective-permute-start.4 = (f32[16,2048]{1,0:T(8,128)S(1)}, f32[16,2048]{1,0:T(8,128)S(1)}, u32[]{:S(2)}, u32[]{:S(2)}) collective-permute-start(f32[16,2048]{1,0:T(8,128)S(1)} %get-tuple-element.49), channel_id=1, source_target_pairs={{0,24},{4,12},{8,16},{12,4},{16,8},{20,28},{24,0},{28,20},{32,56},... | collective-permute-start | bytes 393224 | tf_op jit(solution)/shard_map/ppermute | solution.py:38
  21.6 0.0 collective-permute-done.7.a_got
  21.6 0.0 collective-permute-done.8.b_got
  21.6 0.1 shard_map.61
  21.7 0.9 %collective-permute-start.9 = (f32[16,2048]{1,0:T(8,128)S(1)}, f32[16,2048]{1,0:T(8,128)S(1)}, u32[]{:S(2)}, u32[]{:S(2)}) collective-permute-start(f32[16,2048]{1,0:T(8,128)S(1)} %get-tuple-element.59), channel_id=1, source_target_pairs={{0,24},{4,12},{8,16},{12,4},{16,8},{20,28},{24,0},{28,20},{32,56},... | collective-permute-start | bytes 393224 | tf_op jit(solution)/shard_map/ppermute | solution.py:38
  22.6 0.0 collective-permute-done.12.a_got
  22.6 0.6 %collective-permute-done.13.b_got = f32[32,1024]{1,0:T(8,128)S(1)} collective-permute-done((f32[32,1024]{1,0:T(8,128)S(1)}, f32[32,1024]{1,0:T(8,128)S(1)}, u32[]{:S(2)}, u32[]{:S(2)}) %collective-permute-start.13) | collective-permute-done | bytes 131104 | tf_op jit(solution)/shard_map/ppermute | solution.py:38
  23.1 0.1 shard_map.64
  23.2 2.2 %collective-permute-start.14 = (f32[16,2048]{1,0:T(8,128)S(1)}, f32[16,2048]{1,0:T(8,128)S(1)}, u32[]{:S(2)}, u32[]{:S(2)}) collective-permute-start(f32[16,2048]{1,0:T(8,128)S(1)} %get-tuple-element.69), channel_id=1, source_target_pairs={{0,24},{4,12},{8,16},{12,4},{16,8},{20,28},{24,0},{28,20},{32,56},... | collective-permute-start | bytes 393224 | tf_op jit(solution)/shard_map/ppermute | solution.py:38
  25.4 0.4 collective-permute-done.4
  25.7 0.0 copy-start.1
  25.8 2.7 %collective-permute-done.9 = f32[16,2048]{1,0:T(8,128)S(1)} collective-permute-done((f32[16,2048]{1,0:T(8,128)S(1)}, f32[16,2048]{1,0:T(8,128)S(1)}, u32[]{:S(2)}, u32[]{:S(2)}) %collective-permute-start.9) | collective-permute-done | bytes 131104 | tf_op jit(solution)/shard_map/ppermute | solution.py:38
  28.4 0.0 copy-start.2
  28.4 2.3 %collective-permute-done.14 = f32[16,2048]{1,0:T(8,128)S(1)} collective-permute-done((f32[16,2048]{1,0:T(8,128)S(1)}, f32[16,2048]{1,0:T(8,128)S(1)}, u32[]{:S(2)}, u32[]{:S(2)}) %collective-permute-start.14) | collective-permute-done | bytes 131104 | tf_op jit(solution)/shard_map/ppermute | solution.py:38
  30.8 0.1 reshape.7
  30.9 5.5 %collective-permute-start.15 = (f32[4,6144]{1,0:T(4,128)S(1)}, f32[4,6144]{1,0:T(4,128)S(1)}, u32[]{:S(2)}, u32[]{:S(2)}) collective-permute-start(f32[4,6144]{1,0:T(4,128)S(1)} %get-tuple-element.76), channel_id=1, source_target_pairs={{0,160},{4,100},{8,168},{12,108},{16,176},{20,116},{24,184},{28,12... | collective-permute-start | bytes 294920 | tf_op jit(solution)/shard_map/ppermute | solution.py:38
  36.5 0.1 collective-permute-start.16
  36.5 3.0 %collective-permute-start.17 = (f32[4,6144]{1,0:T(4,128)S(1)}, f32[4,6144]{1,0:T(4,128)S(1)}, u32[]{:S(2)}, u32[]{:S(2)}) collective-permute-start(f32[4,6144]{1,0:T(4,128)S(1)} %get-tuple-element.71), channel_id=1, source_target_pairs={{0,224},{4,36},{8,232},{12,44},{16,240},{20,52},{24,248},{28,60},{... | collective-permute-start | bytes 294920 | tf_op jit(solution)/shard_map/ppermute | solution.py:38
  39.6 0.2 multiply_reduce_fusion.1
  39.7 4.2 %collective-permute-done.17 = f32[4,6144]{1,0:T(4,128)S(1)} collective-permute-done((f32[4,6144]{1,0:T(4,128)S(1)}, f32[4,6144]{1,0:T(4,128)S(1)}, u32[]{:S(2)}, u32[]{:S(2)}) %collective-permute-start.17) | collective-permute-done | bytes 98336 | tf_op jit(solution)/shard_map/ppermute | solution.py:38
  43.9 0.0 collective-permute-done.16
  43.9 0.0 collective-permute-done.15
  43.9 0.2 multiply_reduce_fusion
  44.1 1.3 %collective-permute-start.20 = (f32[4,2]{0,1:T(2,128)S(1)}, f32[4,2]{0,1:T(2,128)S(1)}, u32[]{:S(2)}, u32[]{:S(2)}) collective-permute-start(f32[4,2]{0,1:T(2,128)S(1)} %pad_maximum_fusion.1), channel_id=1, source_target_pairs={{0,2},{1,3},{2,0},{3,1},{4,6},{5,7},{6,4},{7,5},{8,10},{9,11},{10,... | collective-permute-start | bytes 104 | tf_op jit(solution)/shard_map/ppermute | solution.py:255
  45.4 2.2 %collective-permute-start.19 = (f32[4,2]{0,1:T(2,128)S(1)}, f32[4,2]{0,1:T(2,128)S(1)}, u32[]{:S(2)}, u32[]{:S(2)}) collective-permute-start(f32[4,2]{0,1:T(2,128)S(1)} %pad_maximum_fusion.1), channel_id=1, source_target_pairs={{0,3},{1,2},{2,1},{3,0},{4,7},{5,6},{6,5},{7,4},{8,11},{9,10},{10,... | collective-permute-start | bytes 104 | tf_op jit(solution)/shard_map/ppermute | solution.py:255
  47.6 0.1 collective-permute-start.18
  47.7 1.6 %collective-permute-done.20 = f32[4,2]{0,1:T(2,128)S(1)} collective-permute-done((f32[4,2]{0,1:T(2,128)S(1)}, f32[4,2]{0,1:T(2,128)S(1)}, u32[]{:S(2)}, u32[]{:S(2)}) %collective-permute-start.20) | collective-permute-done | bytes 64 | tf_op jit(solution)/shard_map/ppermute | solution.py:255
  49.3 0.9 %collective-permute-done.19 = f32[4,2]{0,1:T(2,128)S(1)} collective-permute-done((f32[4,2]{0,1:T(2,128)S(1)}, f32[4,2]{0,1:T(2,128)S(1)}, u32[]{:S(2)}, u32[]{:S(2)}) %collective-permute-start.19) | collective-permute-done | bytes 64 | tf_op jit(solution)/shard_map/ppermute | solution.py:255
  50.2 1.0 %collective-permute-done.18 = f32[4,2]{0,1:T(2,128)S(1)} collective-permute-done((f32[4,2]{0,1:T(2,128)S(1)}, f32[4,2]{0,1:T(2,128)S(1)}, u32[]{:S(2)}, u32[]{:S(2)}) %collective-permute-start.18) | collective-permute-done | bytes 64 | tf_op jit(solution)/shard_map/ppermute | solution.py:255
  51.2 0.8 %fusion.2 = (f32[4,6144]{1,0:T(4,128)}, f32[4,6144]{1,0:T(4,128)}) fusion(f32[4,6144]{1,0:T(4,128)S(1)} %copy-done.1, f32[4,6144]{1,0:T(4,128)S(1)} %get-tuple-element.75, f32[4]{0:T(128)S(1)} %minimum_bitcast_fusion, f32[4,6144]{1,0:T(4,128)S(1)} %copy-done.2), kind=kLoop, calls=%fused_computation.13 | loop fusion | flops 98304 | bytes 491536 | tf_op jit(solution)/shard_map/sub | solution.py:266
  (11 shorter events, 0.1 us)
Async XLA Ops:
  0.6 1.4 %copy-start = (bf16[1,128,6144]{2,1,0:T(8,128)(2,1)S(1)}, bf16[1,128,6144]{2,1,0:T(8,128)(2,1)}, u32[]{:S(2)}) copy-start(bf16[1,128,6144]{2,1,0:T(8,128)(2,1)} %param.5) | copy-start | bytes 4718596
  2.2 7.2 %collective-permute-start = (f32[4,16,1024]{2,1,0:T(8,128)S(1)}, f32[4,16,1024]{2,1,0:T(8,128)S(1)}, u32[]{:S(2)}, u32[]{:S(2)}) collective-permute-start(f32[4,16,1024]{2,1,0:T(8,128)S(1)} %shard_map.50), channel_id=1, source_target_pairs={{0,32},{4,228},{8,40},{12,236},{16,48},{20,244},{24,56},{28,252},{... | collective-permute-start | bytes 786440 | tf_op jit(solution)/shard_map/ppermute | solution.py:38
  4.3 6.8 %collective-permute-start.1 = (f32[8,8,1024]{2,1,0:T(8,128)S(1)}, f32[8,8,1024]{2,1,0:T(8,128)S(1)}, u32[]{:S(2)}, u32[]{:S(2)}) collective-permute-start(f32[8,8,1024]{2,1,0:T(8,128)S(1)} %shard_map.51), channel_id=1, source_target_pairs={{0,8},{4,28},{8,0},{12,20},{16,24},{20,12},{24,16},{28,4},{32,40},... | collective-permute-start | bytes 786440 | tf_op jit(solution)/shard_map/ppermute | solution.py:38
  6.1 6.5 %collective-permute-start.5 = (f32[4,16,1024]{2,1,0:T(8,128)S(1)}, f32[4,16,1024]{2,1,0:T(8,128)S(1)}, u32[]{:S(2)}, u32[]{:S(2)}) collective-permute-start(f32[4,16,1024]{2,1,0:T(8,128)S(1)} %shard_map.52), channel_id=1, source_target_pairs={{0,32},{4,228},{8,40},{12,236},{16,48},{20,244},{24,56},{28,252},{... | collective-permute-start | bytes 786440 | tf_op jit(solution)/shard_map/ppermute | solution.py:38
  6.4 7.2 %collective-permute-start.6 = (f32[8,8,1024]{2,1,0:T(8,128)S(1)}, f32[8,8,1024]{2,1,0:T(8,128)S(1)}, u32[]{:S(2)}, u32[]{:S(2)}) collective-permute-start(f32[8,8,1024]{2,1,0:T(8,128)S(1)} %shard_map.53), channel_id=1, source_target_pairs={{0,8},{4,28},{8,0},{12,20},{16,24},{20,12},{24,16},{28,4},{32,40},... | collective-permute-start | bytes 786440 | tf_op jit(solution)/shard_map/ppermute | solution.py:38
  7.2 8.1 %collective-permute-start.10 = (f32[4,16,1024]{2,1,0:T(8,128)S(1)}, f32[4,16,1024]{2,1,0:T(8,128)S(1)}, u32[]{:S(2)}, u32[]{:S(2)}) collective-permute-start(f32[4,16,1024]{2,1,0:T(8,128)S(1)} %shard_map.54), channel_id=1, source_target_pairs={{0,32},{4,228},{8,40},{12,236},{16,48},{20,244},{24,56},{28,252},{... | collective-permute-start | bytes 786440 | tf_op jit(solution)/shard_map/ppermute | solution.py:38
  9.4 7.1 %collective-permute-start.11 = (f32[8,8,1024]{2,1,0:T(8,128)S(1)}, f32[8,8,1024]{2,1,0:T(8,128)S(1)}, u32[]{:S(2)}, u32[]{:S(2)}) collective-permute-start(f32[8,8,1024]{2,1,0:T(8,128)S(1)} %shard_map.55), channel_id=1, source_target_pairs={{0,8},{4,28},{8,0},{12,20},{16,24},{20,12},{24,16},{28,4},{32,40},... | collective-permute-start | bytes 786440 | tf_op jit(solution)/shard_map/ppermute | solution.py:38
  11.3 6.8 %collective-permute-start.2 = (f32[32,1024]{1,0:T(8,128)S(1)}, f32[32,1024]{1,0:T(8,128)S(1)}, u32[]{:S(2)}, u32[]{:S(2)}) collective-permute-start(f32[32,1024]{1,0:T(8,128)S(1)} %get-tuple-element.46), channel_id=1, source_target_pairs={{0,32},{4,228},{8,40},{12,236},{16,48},{20,244},{24,56},{28,252},{... | collective-permute-start | bytes 393224 | tf_op jit(solution)/shard_map/ppermute | solution.py:38
  12.5 6.2 %collective-permute-start.3 = (f32[32,1024]{1,0:T(8,128)S(1)}, f32[32,1024]{1,0:T(8,128)S(1)}, u32[]{:S(2)}, u32[]{:S(2)}) collective-permute-start(f32[32,1024]{1,0:T(8,128)S(1)} %get-tuple-element.43), channel_id=1, source_target_pairs={{0,8},{4,28},{8,0},{12,20},{16,24},{20,12},{24,16},{28,4},{32,40},... | collective-permute-start | bytes 393224 | tf_op jit(solution)/shard_map/ppermute | solution.py:38
  13.8 7.8 %collective-permute-start.7 = (f32[32,1024]{1,0:T(8,128)S(1)}, f32[32,1024]{1,0:T(8,128)S(1)}, u32[]{:S(2)}, u32[]{:S(2)}) collective-permute-start(f32[32,1024]{1,0:T(8,128)S(1)} %get-tuple-element.55), channel_id=1, source_target_pairs={{0,32},{4,228},{8,40},{12,236},{16,48},{20,244},{24,56},{28,252},{... | collective-permute-start | bytes 393224 | tf_op jit(solution)/shard_map/ppermute | solution.py:38
  15.3 6.3 %collective-permute-start.8 = (f32[32,1024]{1,0:T(8,128)S(1)}, f32[32,1024]{1,0:T(8,128)S(1)}, u32[]{:S(2)}, u32[]{:S(2)}) collective-permute-start(f32[32,1024]{1,0:T(8,128)S(1)} %get-tuple-element.51), channel_id=1, source_target_pairs={{0,8},{4,28},{8,0},{12,20},{16,24},{20,12},{24,16},{28,4},{32,40},... | collective-permute-start | bytes 393224 | tf_op jit(solution)/shard_map/ppermute | solution.py:38
  16.6 5.9 %collective-permute-start.12 = (f32[32,1024]{1,0:T(8,128)S(1)}, f32[32,1024]{1,0:T(8,128)S(1)}, u32[]{:S(2)}, u32[]{:S(2)}) collective-permute-start(f32[32,1024]{1,0:T(8,128)S(1)} %get-tuple-element.65), channel_id=1, source_target_pairs={{0,32},{4,228},{8,40},{12,236},{16,48},{20,244},{24,56},{28,252},{... | collective-permute-start | bytes 393224 | tf_op jit(solution)/shard_map/ppermute | solution.py:38
  18.1 5.0 %collective-permute-start.13 = (f32[32,1024]{1,0:T(8,128)S(1)}, f32[32,1024]{1,0:T(8,128)S(1)}, u32[]{:S(2)}, u32[]{:S(2)}) collective-permute-start(f32[32,1024]{1,0:T(8,128)S(1)} %get-tuple-element.61), channel_id=1, source_target_pairs={{0,8},{4,28},{8,0},{12,20},{16,24},{20,12},{24,16},{28,4},{32,40},... | collective-permute-start | bytes 393224 | tf_op jit(solution)/shard_map/ppermute | solution.py:38
  18.8 7.0 %collective-permute-start.4 = (f32[16,2048]{1,0:T(8,128)S(1)}, f32[16,2048]{1,0:T(8,128)S(1)}, u32[]{:S(2)}, u32[]{:S(2)}) collective-permute-start(f32[16,2048]{1,0:T(8,128)S(1)} %get-tuple-element.49), channel_id=1, source_target_pairs={{0,24},{4,12},{8,16},{12,4},{16,8},{20,28},{24,0},{28,20},{32,56},... | collective-permute-start | bytes 393224 | tf_op jit(solution)/shard_map/ppermute | solution.py:38
  21.7 6.8 %collective-permute-start.9 = (f32[16,2048]{1,0:T(8,128)S(1)}, f32[16,2048]{1,0:T(8,128)S(1)}, u32[]{:S(2)}, u32[]{:S(2)}) collective-permute-start(f32[16,2048]{1,0:T(8,128)S(1)} %get-tuple-element.59), channel_id=1, source_target_pairs={{0,24},{4,12},{8,16},{12,4},{16,8},{20,28},{24,0},{28,20},{32,56},... | collective-permute-start | bytes 393224 | tf_op jit(solution)/shard_map/ppermute | solution.py:38
  23.2 7.6 %collective-permute-start.14 = (f32[16,2048]{1,0:T(8,128)S(1)}, f32[16,2048]{1,0:T(8,128)S(1)}, u32[]{:S(2)}, u32[]{:S(2)}) collective-permute-start(f32[16,2048]{1,0:T(8,128)S(1)} %get-tuple-element.69), channel_id=1, source_target_pairs={{0,24},{4,12},{8,16},{12,4},{16,8},{20,28},{24,0},{28,20},{32,56},... | collective-permute-start | bytes 393224 | tf_op jit(solution)/shard_map/ppermute | solution.py:38
  25.7 13.8 %copy-start.1 = (f32[4,6144]{1,0:T(4,128)S(1)}, f32[4,6144]{1,0:T(4,128)}, u32[]{:S(2)}) copy-start(f32[4,6144]{1,0:T(4,128)} %param.3) | copy-start | bytes 294916
  28.4 22.8 %copy-start.2 = (f32[4,6144]{1,0:T(4,128)S(1)}, f32[4,6144]{1,0:T(4,128)}, u32[]{:S(2)}) copy-start(f32[4,6144]{1,0:T(4,128)} %param.4) | copy-start | bytes 294916
  30.9 13.0 %collective-permute-start.15 = (f32[4,6144]{1,0:T(4,128)S(1)}, f32[4,6144]{1,0:T(4,128)S(1)}, u32[]{:S(2)}, u32[]{:S(2)}) collective-permute-start(f32[4,6144]{1,0:T(4,128)S(1)} %get-tuple-element.76), channel_id=1, source_target_pairs={{0,160},{4,100},{8,168},{12,108},{16,176},{20,116},{24,184},{28,12... | collective-permute-start | bytes 294920 | tf_op jit(solution)/shard_map/ppermute | solution.py:38
  36.5 7.4 %collective-permute-start.16 = (f32[4,6144]{1,0:T(4,128)S(1)}, f32[4,6144]{1,0:T(4,128)S(1)}, u32[]{:S(2)}, u32[]{:S(2)}) collective-permute-start(f32[4,6144]{1,0:T(4,128)S(1)} %get-tuple-element.70), channel_id=1, source_target_pairs={{0,192},{4,68},{8,200},{12,76},{16,208},{20,84},{24,216},{28,92},{... | collective-permute-start | bytes 294920 | tf_op jit(solution)/shard_map/ppermute | solution.py:38
  36.5 7.4 %collective-permute-start.17 = (f32[4,6144]{1,0:T(4,128)S(1)}, f32[4,6144]{1,0:T(4,128)S(1)}, u32[]{:S(2)}, u32[]{:S(2)}) collective-permute-start(f32[4,6144]{1,0:T(4,128)S(1)} %get-tuple-element.71), channel_id=1, source_target_pairs={{0,224},{4,36},{8,232},{12,44},{16,240},{20,52},{24,248},{28,60},{... | collective-permute-start | bytes 294920 | tf_op jit(solution)/shard_map/ppermute | solution.py:38
  44.1 5.2 %collective-permute-start.20 = (f32[4,2]{0,1:T(2,128)S(1)}, f32[4,2]{0,1:T(2,128)S(1)}, u32[]{:S(2)}, u32[]{:S(2)}) collective-permute-start(f32[4,2]{0,1:T(2,128)S(1)} %pad_maximum_fusion.1), channel_id=1, source_target_pairs={{0,2},{1,3},{2,0},{3,1},{4,6},{5,7},{6,4},{7,5},{8,10},{9,11},{10,... | collective-permute-start | bytes 104 | tf_op jit(solution)/shard_map/ppermute | solution.py:255
  45.4 4.8 %collective-permute-start.19 = (f32[4,2]{0,1:T(2,128)S(1)}, f32[4,2]{0,1:T(2,128)S(1)}, u32[]{:S(2)}, u32[]{:S(2)}) collective-permute-start(f32[4,2]{0,1:T(2,128)S(1)} %pad_maximum_fusion.1), channel_id=1, source_target_pairs={{0,3},{1,2},{2,1},{3,0},{4,7},{5,6},{6,5},{7,4},{8,11},{9,10},{10,... | collective-permute-start | bytes 104 | tf_op jit(solution)/shard_map/ppermute | solution.py:255
  47.6 3.6 %collective-permute-start.18 = (f32[4,2]{0,1:T(2,128)S(1)}, f32[4,2]{0,1:T(2,128)S(1)}, u32[]{:S(2)}, u32[]{:S(2)}) collective-permute-start(f32[4,2]{0,1:T(2,128)S(1)} %pad_maximum_fusion.1), channel_id=1, source_target_pairs={{0,1},{1,0},{2,3},{3,2},{4,5},{5,4},{6,7},{7,6},{8,9},{9,8},{10,11... | collective-permute-start | bytes 104 | tf_op jit(solution)/shard_map/ppermute | solution.py:255

commit v4 on v3

--- a/solution.py
+++ b/solution.py
@@ -13,9 +13,10 @@
 learn_rate = 1.0
 
 NZ, NX, NY, NCORE = 8, 4, 4, 2
-PIECES = 3
+WIDTHS = (1920, 1152)
+UNIT = 3072
 LIMIT = 2 << 20
-CHUNK = 512
+CHUNK = 384
 ORDER = (3, 2, 1)
 COL_ORDER = (1, 3, 2)
 
@@ -188,7 +189,7 @@
     each_chunk(a.shape[1], body)
 
 
-def call(kernel, outs, scratch, *args):
+def call(kernel, outs, scratch, *args, limit=LIMIT):
     vmem = pl.BlockSpec(memory_space=pltpu.VMEM)
     specs = [vmem] * len(args)
     if scratch:
@@ -200,7 +201,7 @@
         out_specs=[vmem] * len(outs),
         out_shape=[pltpu.VMEM(shape, jnp.float32) for shape in outs],
         scratch_shapes=[pltpu.VMEM(scratch, jnp.bfloat16), pltpu.SemaphoreType.DMA((scratch[0],))] if scratch else [],
-        compiler_params=pltpu.CompilerParams(vmem_limit_bytes=LIMIT),
+        compiler_params=pltpu.CompilerParams(vmem_limit_bytes=limit),
         cost_estimate=pl.CostEstimate(flops=1024, bytes_accessed=1024, transcendentals=0),
     )(*args)
 
@@ -219,29 +220,30 @@
 
 def sum_parts(local):
     cols = local.shape[1]
-    n = cols // (2 * PIECES)
-    a_at, b_at = [2 * i * n for i in range(PIECES)], [(2 * i + 1) * n for i in range(PIECES)]
+    widths = [cols // 2 * w // UNIT for w in WIDTHS]
+    a_at = [2 * sum(widths[:i]) for i in range(len(widths))]
+    b_at = [a + w for a, w in zip(a_at, widths)]
     z, x, core, s = place()
     odd = lax.rem(x, 2) == 1
 
     later, a_got, b_got = local, [], []
-    for a, b in zip(a_at, b_at):
+    for a, b, n in zip(a_at, b_at, widths):
+        (out,) = call(functools.partial(give_x_kernel, a), [(NZ, 8, n)], (4, 32, n), later, limit=None if later is local else LIMIT)
+        a_got.append(send_x_first(out))
+        later = after(local, out)
         (out,) = call(functools.partial(give_z_kernel, b), [(4, 16, n)], (4, 16, n), later)
         b_got.append(send_z_pair(out))
         later = after(local, out)
-        (out,) = call(functools.partial(give_x_kernel, a), [(NZ, 8, n)], (4, 32, n), later)
-        a_got.append(send_x_first(out))
-        later = after(local, out)
     a_own, b_own = [], []
-    for i in range(PIECES):
+    for i, n in enumerate(widths):
+        own, out = call(functools.partial(a_kernel, a_at[i]), [(32, n)] * 2, (4, 32, n), later, a_got[i])
+        a_own.append((own, send_z_pair(out)))
+        later = after(local, out)
         own, out = call(functools.partial(b_kernel, b_at[i]), [(32, n)] * 2, (4, 16, n), later, b_got[i])
         b_own.append((own, send_x_first(out)))
         later = after(local, out)
-        own, out = call(functools.partial(a_kernel, a_at[i]), [(32, n)] * 2, (4, 32, n), later, a_got[i])
-        a_own.append((own, send_z_pair(out)))
-        later = after(local, out)
     kept, last = [], None
-    for (a, a_got), (b, b_got) in zip(a_own, b_own):
+    for (a, a_got), (b, b_got), n in zip(a_own, b_own, widths):
         own, out = call(join_kernel, [(16, 2 * n)] * 2, None, a if last is None else after(a, last), a_got, b, b_got)
         kept.append((own, send_x_second(out)))
         last = out

time: 53 us -> 51.6 us (0.974)
  starting transfers between devices: 32 us -> 27.8 us
  waiting for transfers between devices: 14.2 us -> 18 us
  local copies, waits for them, and re-layouts: 1.56 us -> 0.16 us
  Pallas kernels: 2.07 us -> 3.01 us
    ppermute x18 -> x13, starting transfers between devices: 28.5 us -> 24.2 us  [send(): return lax.ppermute(value, ('dp', 'row'), pairs_zx(target))]
    ppermute x18 -> x13, waiting for transfers between devices: 10.7 us -> 14.5 us  [send(): return lax.ppermute(value, ('dp', 'row'), pairs_zx(target))]
    unnamed x6, local copies, waits for them, and re-layouts: 1.41 us -> 0.01 us
    pallas_call x15 -> x10, Pallas kernels: 2.07 us -> 3.01 us  [call(): pl.pallas_call(kernel, in_specs=specs, out_specs=[vmem] * len(outs), out_...]
  transfers between devices with their start and end apart: 21 -> 16, of which waited for: 10 -> 9; matrix products, arithmetic and copies ran while one was open for 0% -> 0% of each run, Pallas kernels for 4% -> 3%
where the time goes in v4:
time: 51.6 us; the launch traced here: 50.9 us
  starting transfers between devices  27.8 us (54%)
  waiting for transfers between devices  18 us (35%)
  Pallas kernels  3.01 us (6%)
  other arithmetic  1.23 us (2%)
  between operations  0.78 us (2%)
    ppermute x13, starting transfers between devices, send(): return lax.ppermute(value, ('dp', 'row'), pairs_zx(target))  24.2 us
    ppermute x13, waiting for transfers between devices, send(): return lax.ppermute(value, ('dp', 'row'), pairs_zx(target))  14.5 us
    ppermute x3, starting transfers between devices, sum_over_col(): lax.ppermute(value, 'col', [(i, i ^ m) for i in range(NY)])  3.57 us
    ppermute x3, waiting for transfers between devices, sum_over_col(): lax.ppermute(value, 'col', [(i, i ^ m) for i in range(NY)])  3.5 us
    pallas_call x10, Pallas kernels, call(): pl.pallas_call(kernel, in_specs=specs, out_specs=[vmem] * len(outs), out_...  3.01 us
  transfers between devices with their start and end apart: 16, of which 9 were waited for; matrix products, arithmetic and copies ran while one was open for 0% of the time, Pallas kernels for 3%

profile of v4, /device:TPU:24, one launch (start us, length us, event | category | flops | bytes accessed | tf_op | source)
XLA Modules:
  0.0 50.9 jit_solution(3080857407658643506)
XLA Ops:
  0.6 0.0 copy-start
  0.6 1.3 %shard_map.50 = f32[8,8,1920]{2,1,0:T(8,128)S(1)} custom-call(bf16[128,6144]{1,0:T(8,128)(2,1)} %bitcast.18), custom_call_target="tpu_custom_call" | custom-call | flops 1024 | bytes 1024 | tf_op jit(solution)/shard_map/pallas_call | solution.py:198
  2.0 1.6 %collective-permute-start = (f32[8,8,1920]{2,1,0:T(8,128)S(1)}, f32[8,8,1920]{2,1,0:T(8,128)S(1)}, u32[]{:S(2)}, u32[]{:S(2)}) collective-permute-start(f32[8,8,1920]{2,1,0:T(8,128)S(1)} %shard_map.50), channel_id=1, source_target_pairs={{0,8},{4,28},{8,0},{12,20},{16,24},{20,12},{24,16},{28,4},{32,40},... | collective-permute-start | bytes 1474568 | tf_op jit(solution)/shard_map/ppermute | solution.py:39
  3.5 0.0 copy-done
  3.5 0.2 shard_map.51
  3.8 2.0 %collective-permute-start.2 = (f32[4,16,1920]{2,1,0:T(8,128)S(1)}, f32[4,16,1920]{2,1,0:T(8,128)S(1)}, u32[]{:S(2)}, u32[]{:S(2)}) collective-permute-start(f32[4,16,1920]{2,1,0:T(8,128)S(1)} %shard_map.51), channel_id=1, source_target_pairs={{0,32},{4,228},{8,40},{12,236},{16,48},{20,244},{24,56},{28,252},{... | collective-permute-start | bytes 1474568 | tf_op jit(solution)/shard_map/ppermute | solution.py:39
  5.8 0.2 shard_map.52
  6.0 0.6 %collective-permute-start.5 = (f32[8,8,1152]{2,1,0:T(8,128)S(1)}, f32[8,8,1152]{2,1,0:T(8,128)S(1)}, u32[]{:S(2)}, u32[]{:S(2)}) collective-permute-start(f32[8,8,1152]{2,1,0:T(8,128)S(1)} %shard_map.52), channel_id=1, source_target_pairs={{0,8},{4,28},{8,0},{12,20},{16,24},{20,12},{24,16},{28,4},{32,40},... | collective-permute-start | bytes 884744 | tf_op jit(solution)/shard_map/ppermute | solution.py:39
  6.6 0.1 shard_map.53
  6.7 0.2 collective-permute-start.7
  6.9 3.9 %collective-permute-done.got = f32[8,8,1920]{2,1,0:T(8,128)S(1)} collective-permute-done((f32[8,8,1920]{2,1,0:T(8,128)S(1)}, f32[8,8,1920]{2,1,0:T(8,128)S(1)}, u32[]{:S(2)}, u32[]{:S(2)}) %collective-permute-start) | collective-permute-done | bytes 491552 | tf_op jit(solution)/shard_map/ppermute | solution.py:39
  10.9 0.3 shard_map.54
  11.2 2.0 %collective-permute-start.1 = (f32[32,1920]{1,0:T(8,128)S(1)}, f32[32,1920]{1,0:T(8,128)S(1)}, u32[]{:S(2)}, u32[]{:S(2)}) collective-permute-start(f32[32,1920]{1,0:T(8,128)S(1)} %get-tuple-element.30), channel_id=1, source_target_pairs={{0,32},{4,228},{8,40},{12,236},{16,48},{20,244},{24,56},{28,252},{... | collective-permute-start | bytes 737288 | tf_op jit(solution)/shard_map/ppermute | solution.py:39
  13.2 0.0 collective-permute-done.2.got
  13.2 0.3 shard_map.55
  13.5 1.6 %collective-permute-start.3 = (f32[32,1920]{1,0:T(8,128)S(1)}, f32[32,1920]{1,0:T(8,128)S(1)}, u32[]{:S(2)}, u32[]{:S(2)}) collective-permute-start(f32[32,1920]{1,0:T(8,128)S(1)} %get-tuple-element.33), channel_id=1, source_target_pairs={{0,8},{4,28},{8,0},{12,20},{16,24},{20,12},{24,16},{28,4},{32,40},... | collective-permute-start | bytes 737288 | tf_op jit(solution)/shard_map/ppermute | solution.py:39
  15.1 0.0 collective-permute-done.5.got
  15.1 0.2 shard_map.57
  15.3 1.0 %collective-permute-start.6 = (f32[32,1152]{1,0:T(8,128)S(1)}, f32[32,1152]{1,0:T(8,128)S(1)}, u32[]{:S(2)}, u32[]{:S(2)}) collective-permute-start(f32[32,1152]{1,0:T(8,128)S(1)} %get-tuple-element.39), channel_id=1, source_target_pairs={{0,32},{4,228},{8,40},{12,236},{16,48},{20,244},{24,56},{28,252},{... | collective-permute-start | bytes 442376 | tf_op jit(solution)/shard_map/ppermute | solution.py:39
  16.3 0.0 collective-permute-done.7.got
  16.3 0.2 shard_map.58
  16.4 1.6 %collective-permute-start.8 = (f32[32,1152]{1,0:T(8,128)S(1)}, f32[32,1152]{1,0:T(8,128)S(1)}, u32[]{:S(2)}, u32[]{:S(2)}) collective-permute-start(f32[32,1152]{1,0:T(8,128)S(1)} %get-tuple-element.42), channel_id=1, source_target_pairs={{0,8},{4,28},{8,0},{12,20},{16,24},{20,12},{24,16},{28,4},{32,40},... | collective-permute-start | bytes 442376 | tf_op jit(solution)/shard_map/ppermute | solution.py:39
  18.0 0.5 collective-permute-done.1.a_got
  18.5 1.3 %collective-permute-done.3.b_got = f32[32,1920]{1,0:T(8,128)S(1)} collective-permute-done((f32[32,1920]{1,0:T(8,128)S(1)}, f32[32,1920]{1,0:T(8,128)S(1)}, u32[]{:S(2)}, u32[]{:S(2)}) %collective-permute-start.3) | collective-permute-done | bytes 245792 | tf_op jit(solution)/shard_map/ppermute | solution.py:39
  19.8 0.1 shard_map.56
  19.9 2.8 %collective-permute-start.4 = (f32[16,3840]{1,0:T(8,128)S(1)}, f32[16,3840]{1,0:T(8,128)S(1)}, u32[]{:S(2)}, u32[]{:S(2)}) collective-permute-start(f32[16,3840]{1,0:T(8,128)S(1)} %get-tuple-element.35), channel_id=1, source_target_pairs={{0,24},{4,12},{8,16},{12,4},{16,8},{20,28},{24,0},{28,20},{32,56},... | collective-permute-start | bytes 737288 | tf_op jit(solution)/shard_map/ppermute | solution.py:39
  22.7 0.0 collective-permute-done.6.a_got
  22.7 0.0 collective-permute-done.8.b_got
  22.7 0.1 shard_map.59
  22.8 1.8 %collective-permute-start.9 = (f32[16,2304]{1,0:T(8,128)S(1)}, f32[16,2304]{1,0:T(8,128)S(1)}, u32[]{:S(2)}, u32[]{:S(2)}) collective-permute-start(f32[16,2304]{1,0:T(8,128)S(1)} %get-tuple-element.45), channel_id=1, source_target_pairs={{0,24},{4,12},{8,16},{12,4},{16,8},{20,28},{24,0},{28,20},{32,56},... | collective-permute-start | bytes 442376 | tf_op jit(solution)/shard_map/ppermute | solution.py:39
  24.6 3.7 %collective-permute-done.4 = f32[16,3840]{1,0:T(8,128)S(1)} collective-permute-done((f32[16,3840]{1,0:T(8,128)S(1)}, f32[16,3840]{1,0:T(8,128)S(1)}, u32[]{:S(2)}, u32[]{:S(2)}) %collective-permute-start.4) | collective-permute-done | bytes 245792 | tf_op jit(solution)/shard_map/ppermute | solution.py:39
  28.3 0.0 copy-start.1
  28.4 0.0 copy-start.2
  28.4 1.5 %collective-permute-done.9 = f32[16,2304]{1,0:T(8,128)S(1)} collective-permute-done((f32[16,2304]{1,0:T(8,128)S(1)}, f32[16,2304]{1,0:T(8,128)S(1)}, u32[]{:S(2)}, u32[]{:S(2)}) %collective-permute-start.9) | collective-permute-done | bytes 147488 | tf_op jit(solution)/shard_map/ppermute | solution.py:39
  30.0 0.1 reshape.7
  30.1 5.4 %collective-permute-start.10 = (f32[4,6144]{1,0:T(4,128)S(1)}, f32[4,6144]{1,0:T(4,128)S(1)}, u32[]{:S(2)}, u32[]{:S(2)}) collective-permute-start(f32[4,6144]{1,0:T(4,128)S(1)} %get-tuple-element.52), channel_id=1, source_target_pairs={{0,160},{4,100},{8,168},{12,108},{16,176},{20,116},{24,184},{28,12... | collective-permute-start | bytes 294920 | tf_op jit(solution)/shard_map/ppermute | solution.py:39
  35.5 0.6 %collective-permute-start.11 = (f32[4,6144]{1,0:T(4,128)S(1)}, f32[4,6144]{1,0:T(4,128)S(1)}, u32[]{:S(2)}, u32[]{:S(2)}) collective-permute-start(f32[4,6144]{1,0:T(4,128)S(1)} %get-tuple-element.46), channel_id=1, source_target_pairs={{0,192},{4,68},{8,200},{12,76},{16,208},{20,84},{24,216},{28,92},{... | collective-permute-start | bytes 294920 | tf_op jit(solution)/shard_map/ppermute | solution.py:39
  36.1 3.1 %collective-permute-start.12 = (f32[4,6144]{1,0:T(4,128)S(1)}, f32[4,6144]{1,0:T(4,128)S(1)}, u32[]{:S(2)}, u32[]{:S(2)}) collective-permute-start(f32[4,6144]{1,0:T(4,128)S(1)} %get-tuple-element.47), channel_id=1, source_target_pairs={{0,224},{4,36},{8,232},{12,44},{16,240},{20,52},{24,248},{28,60},{... | collective-permute-start | bytes 294920 | tf_op jit(solution)/shard_map/ppermute | solution.py:39
  39.2 0.0 copy-done.1
  39.2 0.2 multiply_reduce_fusion.1
  39.4 3.5 %collective-permute-done.12 = f32[4,6144]{1,0:T(4,128)S(1)} collective-permute-done((f32[4,6144]{1,0:T(4,128)S(1)}, f32[4,6144]{1,0:T(4,128)S(1)}, u32[]{:S(2)}, u32[]{:S(2)}) %collective-permute-start.12) | collective-permute-done | bytes 98336 | tf_op jit(solution)/shard_map/ppermute | solution.py:39
  42.8 0.0 collective-permute-done.11
  42.8 0.0 collective-permute-done.10
  42.8 0.2 multiply_reduce_fusion
  43.0 1.3 %collective-permute-start.15 = (f32[4,2]{0,1:T(2,128)S(1)}, f32[4,2]{0,1:T(2,128)S(1)}, u32[]{:S(2)}, u32[]{:S(2)}) collective-permute-start(f32[4,2]{0,1:T(2,128)S(1)} %pad_maximum_fusion.1), channel_id=1, source_target_pairs={{0,2},{1,3},{2,0},{3,1},{4,6},{5,7},{6,4},{7,5},{8,10},{9,11},{10,... | collective-permute-start | bytes 104 | tf_op jit(solution)/shard_map/ppermute | solution.py:257
  44.4 2.2 %collective-permute-start.14 = (f32[4,2]{0,1:T(2,128)S(1)}, f32[4,2]{0,1:T(2,128)S(1)}, u32[]{:S(2)}, u32[]{:S(2)}) collective-permute-start(f32[4,2]{0,1:T(2,128)S(1)} %pad_maximum_fusion.1), channel_id=1, source_target_pairs={{0,3},{1,2},{2,1},{3,0},{4,7},{5,6},{6,5},{7,4},{8,11},{9,10},{10,... | collective-permute-start | bytes 104 | tf_op jit(solution)/shard_map/ppermute | solution.py:257
  46.5 0.1 collective-permute-start.13
  46.6 1.6 %collective-permute-done.15 = f32[4,2]{0,1:T(2,128)S(1)} collective-permute-done((f32[4,2]{0,1:T(2,128)S(1)}, f32[4,2]{0,1:T(2,128)S(1)}, u32[]{:S(2)}, u32[]{:S(2)}) %collective-permute-start.15) | collective-permute-done | bytes 64 | tf_op jit(solution)/shard_map/ppermute | solution.py:257
  48.2 0.9 %collective-permute-done.14 = f32[4,2]{0,1:T(2,128)S(1)} collective-permute-done((f32[4,2]{0,1:T(2,128)S(1)}, f32[4,2]{0,1:T(2,128)S(1)}, u32[]{:S(2)}, u32[]{:S(2)}) %collective-permute-start.14) | collective-permute-done | bytes 64 | tf_op jit(solution)/shard_map/ppermute | solution.py:257
  49.1 1.0 %collective-permute-done.13 = f32[4,2]{0,1:T(2,128)S(1)} collective-permute-done((f32[4,2]{0,1:T(2,128)S(1)}, f32[4,2]{0,1:T(2,128)S(1)}, u32[]{:S(2)}, u32[]{:S(2)}) %collective-permute-start.13) | collective-permute-done | bytes 64 | tf_op jit(solution)/shard_map/ppermute | solution.py:257
  50.1 0.0 copy-done.2
  50.1 0.8 %fusion.2 = (f32[4,6144]{1,0:T(4,128)}, f32[4,6144]{1,0:T(4,128)}) fusion(f32[4,6144]{1,0:T(4,128)S(1)} %copy-done.1, f32[4,6144]{1,0:T(4,128)S(1)} %get-tuple-element.51, f32[4]{0:T(128)S(1)} %minimum_bitcast_fusion, f32[4,6144]{1,0:T(4,128)S(1)} %copy-done.2), kind=kLoop, calls=%fused_computation.13 | loop fusion | flops 98304 | bytes 491536 | tf_op jit(solution)/shard_map/sub | solution.py:268
  (7 shorter events, 0.1 us)
Async XLA Ops:
  0.6 2.9 %copy-start = (bf16[1,128,6144]{2,1,0:T(8,128)(2,1)S(1)}, bf16[1,128,6144]{2,1,0:T(8,128)(2,1)}, u32[]{:S(2)}) copy-start(bf16[1,128,6144]{2,1,0:T(8,128)(2,1)} %param.5) | copy-start | bytes 4718596
  2.0 8.9 %collective-permute-start = (f32[8,8,1920]{2,1,0:T(8,128)S(1)}, f32[8,8,1920]{2,1,0:T(8,128)S(1)}, u32[]{:S(2)}, u32[]{:S(2)}) collective-permute-start(f32[8,8,1920]{2,1,0:T(8,128)S(1)} %shard_map.50), channel_id=1, source_target_pairs={{0,8},{4,28},{8,0},{12,20},{16,24},{20,12},{24,16},{28,4},{32,40},... | collective-permute-start | bytes 1474568 | tf_op jit(solution)/shard_map/ppermute | solution.py:39
  3.8 9.4 %collective-permute-start.2 = (f32[4,16,1920]{2,1,0:T(8,128)S(1)}, f32[4,16,1920]{2,1,0:T(8,128)S(1)}, u32[]{:S(2)}, u32[]{:S(2)}) collective-permute-start(f32[4,16,1920]{2,1,0:T(8,128)S(1)} %shard_map.51), channel_id=1, source_target_pairs={{0,32},{4,228},{8,40},{12,236},{16,48},{20,244},{24,56},{28,252},{... | collective-permute-start | bytes 1474568 | tf_op jit(solution)/shard_map/ppermute | solution.py:39
  6.0 9.1 %collective-permute-start.5 = (f32[8,8,1152]{2,1,0:T(8,128)S(1)}, f32[8,8,1152]{2,1,0:T(8,128)S(1)}, u32[]{:S(2)}, u32[]{:S(2)}) collective-permute-start(f32[8,8,1152]{2,1,0:T(8,128)S(1)} %shard_map.52), channel_id=1, source_target_pairs={{0,8},{4,28},{8,0},{12,20},{16,24},{20,12},{24,16},{28,4},{32,40},... | collective-permute-start | bytes 884744 | tf_op jit(solution)/shard_map/ppermute | solution.py:39
  6.7 9.5 %collective-permute-start.7 = (f32[4,16,1152]{2,1,0:T(8,128)S(1)}, f32[4,16,1152]{2,1,0:T(8,128)S(1)}, u32[]{:S(2)}, u32[]{:S(2)}) collective-permute-start(f32[4,16,1152]{2,1,0:T(8,128)S(1)} %shard_map.53), channel_id=1, source_target_pairs={{0,32},{4,228},{8,40},{12,236},{16,48},{20,244},{24,56},{28,252},{... | collective-permute-start | bytes 884744 | tf_op jit(solution)/shard_map/ppermute | solution.py:39
  11.2 7.3 %collective-permute-start.1 = (f32[32,1920]{1,0:T(8,128)S(1)}, f32[32,1920]{1,0:T(8,128)S(1)}, u32[]{:S(2)}, u32[]{:S(2)}) collective-permute-start(f32[32,1920]{1,0:T(8,128)S(1)} %get-tuple-element.30), channel_id=1, source_target_pairs={{0,32},{4,228},{8,40},{12,236},{16,48},{20,244},{24,56},{28,252},{... | collective-permute-start | bytes 737288 | tf_op jit(solution)/shard_map/ppermute | solution.py:39
  13.5 6.3 %collective-permute-start.3 = (f32[32,1920]{1,0:T(8,128)S(1)}, f32[32,1920]{1,0:T(8,128)S(1)}, u32[]{:S(2)}, u32[]{:S(2)}) collective-permute-start(f32[32,1920]{1,0:T(8,128)S(1)} %get-tuple-element.33), channel_id=1, source_target_pairs={{0,8},{4,28},{8,0},{12,20},{16,24},{20,12},{24,16},{28,4},{32,40},... | collective-permute-start | bytes 737288 | tf_op jit(solution)/shard_map/ppermute | solution.py:39
  15.3 7.5 %collective-permute-start.6 = (f32[32,1152]{1,0:T(8,128)S(1)}, f32[32,1152]{1,0:T(8,128)S(1)}, u32[]{:S(2)}, u32[]{:S(2)}) collective-permute-start(f32[32,1152]{1,0:T(8,128)S(1)} %get-tuple-element.39), channel_id=1, source_target_pairs={{0,32},{4,228},{8,40},{12,236},{16,48},{20,244},{24,56},{28,252},{... | collective-permute-start | bytes 442376 | tf_op jit(solution)/shard_map/ppermute | solution.py:39
  16.4 6.3 %collective-permute-start.8 = (f32[32,1152]{1,0:T(8,128)S(1)}, f32[32,1152]{1,0:T(8,128)S(1)}, u32[]{:S(2)}, u32[]{:S(2)}) collective-permute-start(f32[32,1152]{1,0:T(8,128)S(1)} %get-tuple-element.42), channel_id=1, source_target_pairs={{0,8},{4,28},{8,0},{12,20},{16,24},{20,12},{24,16},{28,4},{32,40},... | collective-permute-start | bytes 442376 | tf_op jit(solution)/shard_map/ppermute | solution.py:39
  19.9 8.4 %collective-permute-start.4 = (f32[16,3840]{1,0:T(8,128)S(1)}, f32[16,3840]{1,0:T(8,128)S(1)}, u32[]{:S(2)}, u32[]{:S(2)}) collective-permute-start(f32[16,3840]{1,0:T(8,128)S(1)} %get-tuple-element.35), channel_id=1, source_target_pairs={{0,24},{4,12},{8,16},{12,4},{16,8},{20,28},{24,0},{28,20},{32,56},... | collective-permute-start | bytes 737288 | tf_op jit(solution)/shard_map/ppermute | solution.py:39
  22.8 7.1 %collective-permute-start.9 = (f32[16,2304]{1,0:T(8,128)S(1)}, f32[16,2304]{1,0:T(8,128)S(1)}, u32[]{:S(2)}, u32[]{:S(2)}) collective-permute-start(f32[16,2304]{1,0:T(8,128)S(1)} %get-tuple-element.45), channel_id=1, source_target_pairs={{0,24},{4,12},{8,16},{12,4},{16,8},{20,28},{24,0},{28,20},{32,56},... | collective-permute-start | bytes 442376 | tf_op jit(solution)/shard_map/ppermute | solution.py:39
  28.3 10.8 %copy-start.1 = (f32[4,6144]{1,0:T(4,128)S(1)}, f32[4,6144]{1,0:T(4,128)}, u32[]{:S(2)}) copy-start(f32[4,6144]{1,0:T(4,128)} %param.3) | copy-start | bytes 294916
  28.4 21.8 %copy-start.2 = (f32[4,6144]{1,0:T(4,128)S(1)}, f32[4,6144]{1,0:T(4,128)}, u32[]{:S(2)}) copy-start(f32[4,6144]{1,0:T(4,128)} %param.4) | copy-start | bytes 294916
  30.1 12.7 %collective-permute-start.10 = (f32[4,6144]{1,0:T(4,128)S(1)}, f32[4,6144]{1,0:T(4,128)S(1)}, u32[]{:S(2)}, u32[]{:S(2)}) collective-permute-start(f32[4,6144]{1,0:T(4,128)S(1)} %get-tuple-element.52), channel_id=1, source_target_pairs={{0,160},{4,100},{8,168},{12,108},{16,176},{20,116},{24,184},{28,12... | collective-permute-start | bytes 294920 | tf_op jit(solution)/shard_map/ppermute | solution.py:39
  35.5 7.3 %collective-permute-start.11 = (f32[4,6144]{1,0:T(4,128)S(1)}, f32[4,6144]{1,0:T(4,128)S(1)}, u32[]{:S(2)}, u32[]{:S(2)}) collective-permute-start(f32[4,6144]{1,0:T(4,128)S(1)} %get-tuple-element.46), channel_id=1, source_target_pairs={{0,192},{4,68},{8,200},{12,76},{16,208},{20,84},{24,216},{28,92},{... | collective-permute-start | bytes 294920 | tf_op jit(solution)/shard_map/ppermute | solution.py:39
  36.1 6.8 %collective-permute-start.12 = (f32[4,6144]{1,0:T(4,128)S(1)}, f32[4,6144]{1,0:T(4,128)S(1)}, u32[]{:S(2)}, u32[]{:S(2)}) collective-permute-start(f32[4,6144]{1,0:T(4,128)S(1)} %get-tuple-element.47), channel_id=1, source_target_pairs={{0,224},{4,36},{8,232},{12,44},{16,240},{20,52},{24,248},{28,60},{... | collective-permute-start | bytes 294920 | tf_op jit(solution)/shard_map/ppermute | solution.py:39
  43.0 5.2 %collective-permute-start.15 = (f32[4,2]{0,1:T(2,128)S(1)}, f32[4,2]{0,1:T(2,128)S(1)}, u32[]{:S(2)}, u32[]{:S(2)}) collective-permute-start(f32[4,2]{0,1:T(2,128)S(1)} %pad_maximum_fusion.1), channel_id=1, source_target_pairs={{0,2},{1,3},{2,0},{3,1},{4,6},{5,7},{6,4},{7,5},{8,10},{9,11},{10,... | collective-permute-start | bytes 104 | tf_op jit(solution)/shard_map/ppermute | solution.py:257
  44.4 4.8 %collective-permute-start.14 = (f32[4,2]{0,1:T(2,128)S(1)}, f32[4,2]{0,1:T(2,128)S(1)}, u32[]{:S(2)}, u32[]{:S(2)}) collective-permute-start(f32[4,2]{0,1:T(2,128)S(1)} %pad_maximum_fusion.1), channel_id=1, source_target_pairs={{0,3},{1,2},{2,1},{3,0},{4,7},{5,6},{6,5},{7,4},{8,11},{9,10},{10,... | collective-permute-start | bytes 104 | tf_op jit(solution)/shard_map/ppermute | solution.py:257
  46.5 3.6 %collective-permute-start.13 = (f32[4,2]{0,1:T(2,128)S(1)}, f32[4,2]{0,1:T(2,128)S(1)}, u32[]{:S(2)}, u32[]{:S(2)}) collective-permute-start(f32[4,2]{0,1:T(2,128)S(1)} %pad_maximum_fusion.1), channel_id=1, source_target_pairs={{0,1},{1,0},{2,3},{3,2},{4,5},{5,4},{6,7},{7,6},{8,9},{9,8},{10,11... | collective-permute-start | bytes 104 | tf_op jit(solution)/shard_map/ppermute | solution.py:257

commit v5 on v4

--- a/solution.py
+++ b/solution.py
@@ -109,16 +109,16 @@
     ]
     for copy in copies:
         copy.start()
-    for copy in copies:
-        copy.wait()
-
-    def body(first, n):
+
+    def body(j, first, n):
         high = jnp.broadcast_to(jnp.where(x_high(x, core), 1, 0), (8, n)) == 0
-        for k in range(NZ):
+        for k in (2 * j, 2 * j + 1):
             rows = buf[k // 2, k % 2 * 16 : k % 2 * 16 + 16, pl.ds(first, n)].astype(jnp.float32)
             out[k, :, pl.ds(first, n)] = jnp.where(high, rows[8:], rows[:8])
 
-    each_chunk(buf.shape[2], body)
+    for j, copy in enumerate(copies):
+        copy.wait()
+        each_chunk(buf.shape[2], functools.partial(body, j))
 
 
 def b_kernel(start, src, got, own, out, buf, sem):

time: 51.6 us -> 51.6 us (level)
  no operation moved by 1% of the time
where the time goes in v5:
time: 51.6 us; the launch traced here: 50.9 us
  starting transfers between devices  27.7 us (54%)
  waiting for transfers between devices  18 us (35%)
  Pallas kernels  2.99 us (6%)
  other arithmetic  1.23 us (2%)
  between operations  0.78 us (2%)
    ppermute x13, starting transfers between devices, send(): return lax.ppermute(value, ('dp', 'row'), pairs_zx(target))  24.1 us
    ppermute x13, waiting for transfers between devices, send(): return lax.ppermute(value, ('dp', 'row'), pairs_zx(target))  14.5 us
    ppermute x3, starting transfers between devices, sum_over_col(): lax.ppermute(value, 'col', [(i, i ^ m) for i in range(NY)])  3.57 us
    ppermute x3, waiting for transfers between devices, sum_over_col(): lax.ppermute(value, 'col', [(i, i ^ m) for i in range(NY)])  3.5 us
    pallas_call x10, Pallas kernels, call(): pl.pallas_call(kernel, in_specs=specs, out_specs=[vmem] * len(outs), out_...  2.99 us
  transfers between devices with their start and end apart: 16, of which 9 were waited for; matrix products, arithmetic and copies ran while one was open for 0% of the time, Pallas kernels for 3%

profile of v5, /device:TPU:24, one launch (start us, length us, event | category | flops | bytes accessed | tf_op | source)
XLA Modules:
  0.0 50.9 jit_solution(15508402594535502483)
XLA Ops:
  0.6 0.0 copy-start
  0.6 1.3 %shard_map.50 = f32[8,8,1920]{2,1,0:T(8,128)S(1)} custom-call(bf16[128,6144]{1,0:T(8,128)(2,1)} %bitcast.18), custom_call_target="tpu_custom_call" | custom-call | flops 1024 | bytes 1024 | tf_op jit(solution)/shard_map/pallas_call | solution.py:198
  1.9 1.6 %collective-permute-start = (f32[8,8,1920]{2,1,0:T(8,128)S(1)}, f32[8,8,1920]{2,1,0:T(8,128)S(1)}, u32[]{:S(2)}, u32[]{:S(2)}) collective-permute-start(f32[8,8,1920]{2,1,0:T(8,128)S(1)} %shard_map.50), channel_id=1, source_target_pairs={{0,8},{4,28},{8,0},{12,20},{16,24},{20,12},{24,16},{28,4},{32,40},... | collective-permute-start | bytes 1474568 | tf_op jit(solution)/shard_map/ppermute | solution.py:39
  3.5 0.0 copy-done
  3.5 0.2 shard_map.51
  3.7 2.0 %collective-permute-start.2 = (f32[4,16,1920]{2,1,0:T(8,128)S(1)}, f32[4,16,1920]{2,1,0:T(8,128)S(1)}, u32[]{:S(2)}, u32[]{:S(2)}) collective-permute-start(f32[4,16,1920]{2,1,0:T(8,128)S(1)} %shard_map.51), channel_id=1, source_target_pairs={{0,32},{4,228},{8,40},{12,236},{16,48},{20,244},{24,56},{28,252},{... | collective-permute-start | bytes 1474568 | tf_op jit(solution)/shard_map/ppermute | solution.py:39
  5.7 0.2 shard_map.52
  5.9 0.6 %collective-permute-start.5 = (f32[8,8,1152]{2,1,0:T(8,128)S(1)}, f32[8,8,1152]{2,1,0:T(8,128)S(1)}, u32[]{:S(2)}, u32[]{:S(2)}) collective-permute-start(f32[8,8,1152]{2,1,0:T(8,128)S(1)} %shard_map.52), channel_id=1, source_target_pairs={{0,8},{4,28},{8,0},{12,20},{16,24},{20,12},{24,16},{28,4},{32,40},... | collective-permute-start | bytes 884744 | tf_op jit(solution)/shard_map/ppermute | solution.py:39
  6.6 0.1 shard_map.53
  6.7 0.2 collective-permute-start.7
  6.9 3.9 %collective-permute-done.got = f32[8,8,1920]{2,1,0:T(8,128)S(1)} collective-permute-done((f32[8,8,1920]{2,1,0:T(8,128)S(1)}, f32[8,8,1920]{2,1,0:T(8,128)S(1)}, u32[]{:S(2)}, u32[]{:S(2)}) %collective-permute-start) | collective-permute-done | bytes 491552 | tf_op jit(solution)/shard_map/ppermute | solution.py:39
  10.8 0.3 shard_map.54
  11.1 2.0 %collective-permute-start.1 = (f32[32,1920]{1,0:T(8,128)S(1)}, f32[32,1920]{1,0:T(8,128)S(1)}, u32[]{:S(2)}, u32[]{:S(2)}) collective-permute-start(f32[32,1920]{1,0:T(8,128)S(1)} %get-tuple-element.30), channel_id=1, source_target_pairs={{0,32},{4,228},{8,40},{12,236},{16,48},{20,244},{24,56},{28,252},{... | collective-permute-start | bytes 737288 | tf_op jit(solution)/shard_map/ppermute | solution.py:39
  13.1 0.0 collective-permute-done.2.got
  13.1 0.3 shard_map.55
  13.4 1.6 %collective-permute-start.3 = (f32[32,1920]{1,0:T(8,128)S(1)}, f32[32,1920]{1,0:T(8,128)S(1)}, u32[]{:S(2)}, u32[]{:S(2)}) collective-permute-start(f32[32,1920]{1,0:T(8,128)S(1)} %get-tuple-element.33), channel_id=1, source_target_pairs={{0,8},{4,28},{8,0},{12,20},{16,24},{20,12},{24,16},{28,4},{32,40},... | collective-permute-start | bytes 737288 | tf_op jit(solution)/shard_map/ppermute | solution.py:39
  15.0 0.0 collective-permute-done.5.got
  15.0 0.2 shard_map.57
  15.2 1.0 %collective-permute-start.6 = (f32[32,1152]{1,0:T(8,128)S(1)}, f32[32,1152]{1,0:T(8,128)S(1)}, u32[]{:S(2)}, u32[]{:S(2)}) collective-permute-start(f32[32,1152]{1,0:T(8,128)S(1)} %get-tuple-element.39), channel_id=1, source_target_pairs={{0,32},{4,228},{8,40},{12,236},{16,48},{20,244},{24,56},{28,252},{... | collective-permute-start | bytes 442376 | tf_op jit(solution)/shard_map/ppermute | solution.py:39
  16.2 0.0 collective-permute-done.7.got
  16.2 0.2 shard_map.58
  16.4 1.6 %collective-permute-start.8 = (f32[32,1152]{1,0:T(8,128)S(1)}, f32[32,1152]{1,0:T(8,128)S(1)}, u32[]{:S(2)}, u32[]{:S(2)}) collective-permute-start(f32[32,1152]{1,0:T(8,128)S(1)} %get-tuple-element.42), channel_id=1, source_target_pairs={{0,8},{4,28},{8,0},{12,20},{16,24},{20,12},{24,16},{28,4},{32,40},... | collective-permute-start | bytes 442376 | tf_op jit(solution)/shard_map/ppermute | solution.py:39
  18.0 0.5 collective-permute-done.1.a_got
  18.4 1.3 %collective-permute-done.3.b_got = f32[32,1920]{1,0:T(8,128)S(1)} collective-permute-done((f32[32,1920]{1,0:T(8,128)S(1)}, f32[32,1920]{1,0:T(8,128)S(1)}, u32[]{:S(2)}, u32[]{:S(2)}) %collective-permute-start.3) | collective-permute-done | bytes 245792 | tf_op jit(solution)/shard_map/ppermute | solution.py:39
  19.7 0.1 shard_map.56
  19.8 2.8 %collective-permute-start.4 = (f32[16,3840]{1,0:T(8,128)S(1)}, f32[16,3840]{1,0:T(8,128)S(1)}, u32[]{:S(2)}, u32[]{:S(2)}) collective-permute-start(f32[16,3840]{1,0:T(8,128)S(1)} %get-tuple-element.35), channel_id=1, source_target_pairs={{0,24},{4,12},{8,16},{12,4},{16,8},{20,28},{24,0},{28,20},{32,56},... | collective-permute-start | bytes 737288 | tf_op jit(solution)/shard_map/ppermute | solution.py:39
  22.7 0.0 collective-permute-done.6.a_got
  22.7 0.0 collective-permute-done.8.b_got
  22.7 0.1 shard_map.59
  22.8 1.8 %collective-permute-start.9 = (f32[16,2304]{1,0:T(8,128)S(1)}, f32[16,2304]{1,0:T(8,128)S(1)}, u32[]{:S(2)}, u32[]{:S(2)}) collective-permute-start(f32[16,2304]{1,0:T(8,128)S(1)} %get-tuple-element.45), channel_id=1, source_target_pairs={{0,24},{4,12},{8,16},{12,4},{16,8},{20,28},{24,0},{28,20},{32,56},... | collective-permute-start | bytes 442376 | tf_op jit(solution)/shard_map/ppermute | solution.py:39
  24.5 3.8 %collective-permute-done.4 = f32[16,3840]{1,0:T(8,128)S(1)} collective-permute-done((f32[16,3840]{1,0:T(8,128)S(1)}, f32[16,3840]{1,0:T(8,128)S(1)}, u32[]{:S(2)}, u32[]{:S(2)}) %collective-permute-start.4) | collective-permute-done | bytes 245792 | tf_op jit(solution)/shard_map/ppermute | solution.py:39
  28.4 0.0 copy-start.1
  28.4 0.0 copy-start.2
  28.4 1.5 %collective-permute-done.9 = f32[16,2304]{1,0:T(8,128)S(1)} collective-permute-done((f32[16,2304]{1,0:T(8,128)S(1)}, f32[16,2304]{1,0:T(8,128)S(1)}, u32[]{:S(2)}, u32[]{:S(2)}) %collective-permute-start.9) | collective-permute-done | bytes 147488 | tf_op jit(solution)/shard_map/ppermute | solution.py:39
  30.0 0.1 reshape.7
  30.2 5.3 %collective-permute-start.10 = (f32[4,6144]{1,0:T(4,128)S(1)}, f32[4,6144]{1,0:T(4,128)S(1)}, u32[]{:S(2)}, u32[]{:S(2)}) collective-permute-start(f32[4,6144]{1,0:T(4,128)S(1)} %get-tuple-element.52), channel_id=1, source_target_pairs={{0,160},{4,100},{8,168},{12,108},{16,176},{20,116},{24,184},{28,12... | collective-permute-start | bytes 294920 | tf_op jit(solution)/shard_map/ppermute | solution.py:39
  35.4 0.6 %collective-permute-start.11 = (f32[4,6144]{1,0:T(4,128)S(1)}, f32[4,6144]{1,0:T(4,128)S(1)}, u32[]{:S(2)}, u32[]{:S(2)}) collective-permute-start(f32[4,6144]{1,0:T(4,128)S(1)} %get-tuple-element.46), channel_id=1, source_target_pairs={{0,192},{4,68},{8,200},{12,76},{16,208},{20,84},{24,216},{28,92},{... | collective-permute-start | bytes 294920 | tf_op jit(solution)/shard_map/ppermute | solution.py:39
  36.0 3.1 %collective-permute-start.12 = (f32[4,6144]{1,0:T(4,128)S(1)}, f32[4,6144]{1,0:T(4,128)S(1)}, u32[]{:S(2)}, u32[]{:S(2)}) collective-permute-start(f32[4,6144]{1,0:T(4,128)S(1)} %get-tuple-element.47), channel_id=1, source_target_pairs={{0,224},{4,36},{8,232},{12,44},{16,240},{20,52},{24,248},{28,60},{... | collective-permute-start | bytes 294920 | tf_op jit(solution)/shard_map/ppermute | solution.py:39
  39.1 0.0 copy-done.1
  39.1 0.2 multiply_reduce_fusion.1
  39.3 3.5 %collective-permute-done.12 = f32[4,6144]{1,0:T(4,128)S(1)} collective-permute-done((f32[4,6144]{1,0:T(4,128)S(1)}, f32[4,6144]{1,0:T(4,128)S(1)}, u32[]{:S(2)}, u32[]{:S(2)}) %collective-permute-start.12) | collective-permute-done | bytes 98336 | tf_op jit(solution)/shard_map/ppermute | solution.py:39
  42.8 0.0 collective-permute-done.11
  42.8 0.0 collective-permute-done.10
  42.8 0.2 multiply_reduce_fusion
  43.0 1.3 %collective-permute-start.15 = (f32[4,2]{0,1:T(2,128)S(1)}, f32[4,2]{0,1:T(2,128)S(1)}, u32[]{:S(2)}, u32[]{:S(2)}) collective-permute-start(f32[4,2]{0,1:T(2,128)S(1)} %pad_maximum_fusion.1), channel_id=1, source_target_pairs={{0,2},{1,3},{2,0},{3,1},{4,6},{5,7},{6,4},{7,5},{8,10},{9,11},{10,... | collective-permute-start | bytes 104 | tf_op jit(solution)/shard_map/ppermute | solution.py:257
  44.3 2.2 %collective-permute-start.14 = (f32[4,2]{0,1:T(2,128)S(1)}, f32[4,2]{0,1:T(2,128)S(1)}, u32[]{:S(2)}, u32[]{:S(2)}) collective-permute-start(f32[4,2]{0,1:T(2,128)S(1)} %pad_maximum_fusion.1), channel_id=1, source_target_pairs={{0,3},{1,2},{2,1},{3,0},{4,7},{5,6},{6,5},{7,4},{8,11},{9,10},{10,... | collective-permute-start | bytes 104 | tf_op jit(solution)/shard_map/ppermute | solution.py:257
  46.5 0.1 collective-permute-start.13
  46.5 1.6 %collective-permute-done.15 = f32[4,2]{0,1:T(2,128)S(1)} collective-permute-done((f32[4,2]{0,1:T(2,128)S(1)}, f32[4,2]{0,1:T(2,128)S(1)}, u32[]{:S(2)}, u32[]{:S(2)}) %collective-permute-start.15) | collective-permute-done | bytes 64 | tf_op jit(solution)/shard_map/ppermute | solution.py:257
  48.1 0.9 %collective-permute-done.14 = f32[4,2]{0,1:T(2,128)S(1)} collective-permute-done((f32[4,2]{0,1:T(2,128)S(1)}, f32[4,2]{0,1:T(2,128)S(1)}, u32[]{:S(2)}, u32[]{:S(2)}) %collective-permute-start.14) | collective-permute-done | bytes 64 | tf_op jit(solution)/shard_map/ppermute | solution.py:257
  49.1 1.0 %collective-permute-done.13 = f32[4,2]{0,1:T(2,128)S(1)} collective-permute-done((f32[4,2]{0,1:T(2,128)S(1)}, f32[4,2]{0,1:T(2,128)S(1)}, u32[]{:S(2)}, u32[]{:S(2)}) %collective-permute-start.13) | collective-permute-done | bytes 64 | tf_op jit(solution)/shard_map/ppermute | solution.py:257
  50.1 0.0 copy-done.2
  50.1 0.8 %fusion.2 = (f32[4,6144]{1,0:T(4,128)}, f32[4,6144]{1,0:T(4,128)}) fusion(f32[4,6144]{1,0:T(4,128)S(1)} %copy-done.1, f32[4,6144]{1,0:T(4,128)S(1)} %get-tuple-element.51, f32[4]{0:T(128)S(1)} %minimum_bitcast_fusion, f32[4,6144]{1,0:T(4,128)S(1)} %copy-done.2), kind=kLoop, calls=%fused_computation.13 | loop fusion | flops 98304 | bytes 491536 | tf_op jit(solution)/shard_map/sub | solution.py:268
  (7 shorter events, 0.1 us)
Async XLA Ops:
  0.6 2.9 %copy-start = (bf16[1,128,6144]{2,1,0:T(8,128)(2,1)S(1)}, bf16[1,128,6144]{2,1,0:T(8,128)(2,1)}, u32[]{:S(2)}) copy-start(bf16[1,128,6144]{2,1,0:T(8,128)(2,1)} %param.5) | copy-start | bytes 4718596
  1.9 8.9 %collective-permute-start = (f32[8,8,1920]{2,1,0:T(8,128)S(1)}, f32[8,8,1920]{2,1,0:T(8,128)S(1)}, u32[]{:S(2)}, u32[]{:S(2)}) collective-permute-start(f32[8,8,1920]{2,1,0:T(8,128)S(1)} %shard_map.50), channel_id=1, source_target_pairs={{0,8},{4,28},{8,0},{12,20},{16,24},{20,12},{24,16},{28,4},{32,40},... | collective-permute-start | bytes 1474568 | tf_op jit(solution)/shard_map/ppermute | solution.py:39
  3.7 9.4 %collective-permute-start.2 = (f32[4,16,1920]{2,1,0:T(8,128)S(1)}, f32[4,16,1920]{2,1,0:T(8,128)S(1)}, u32[]{:S(2)}, u32[]{:S(2)}) collective-permute-start(f32[4,16,1920]{2,1,0:T(8,128)S(1)} %shard_map.51), channel_id=1, source_target_pairs={{0,32},{4,228},{8,40},{12,236},{16,48},{20,244},{24,56},{28,252},{... | collective-permute-start | bytes 1474568 | tf_op jit(solution)/shard_map/ppermute | solution.py:39
  5.9 9.1 %collective-permute-start.5 = (f32[8,8,1152]{2,1,0:T(8,128)S(1)}, f32[8,8,1152]{2,1,0:T(8,128)S(1)}, u32[]{:S(2)}, u32[]{:S(2)}) collective-permute-start(f32[8,8,1152]{2,1,0:T(8,128)S(1)} %shard_map.52), channel_id=1, source_target_pairs={{0,8},{4,28},{8,0},{12,20},{16,24},{20,12},{24,16},{28,4},{32,40},... | collective-permute-start | bytes 884744 | tf_op jit(solution)/shard_map/ppermute | solution.py:39
  6.7 9.5 %collective-permute-start.7 = (f32[4,16,1152]{2,1,0:T(8,128)S(1)}, f32[4,16,1152]{2,1,0:T(8,128)S(1)}, u32[]{:S(2)}, u32[]{:S(2)}) collective-permute-start(f32[4,16,1152]{2,1,0:T(8,128)S(1)} %shard_map.53), channel_id=1, source_target_pairs={{0,32},{4,228},{8,40},{12,236},{16,48},{20,244},{24,56},{28,252},{... | collective-permute-start | bytes 884744 | tf_op jit(solution)/shard_map/ppermute | solution.py:39
  11.1 7.3 %collective-permute-start.1 = (f32[32,1920]{1,0:T(8,128)S(1)}, f32[32,1920]{1,0:T(8,128)S(1)}, u32[]{:S(2)}, u32[]{:S(2)}) collective-permute-start(f32[32,1920]{1,0:T(8,128)S(1)} %get-tuple-element.30), channel_id=1, source_target_pairs={{0,32},{4,228},{8,40},{12,236},{16,48},{20,244},{24,56},{28,252},{... | collective-permute-start | bytes 737288 | tf_op jit(solution)/shard_map/ppermute | solution.py:39
  13.4 6.3 %collective-permute-start.3 = (f32[32,1920]{1,0:T(8,128)S(1)}, f32[32,1920]{1,0:T(8,128)S(1)}, u32[]{:S(2)}, u32[]{:S(2)}) collective-permute-start(f32[32,1920]{1,0:T(8,128)S(1)} %get-tuple-element.33), channel_id=1, source_target_pairs={{0,8},{4,28},{8,0},{12,20},{16,24},{20,12},{24,16},{28,4},{32,40},... | collective-permute-start | bytes 737288 | tf_op jit(solution)/shard_map/ppermute | solution.py:39
  15.2 7.5 %collective-permute-start.6 = (f32[32,1152]{1,0:T(8,128)S(1)}, f32[32,1152]{1,0:T(8,128)S(1)}, u32[]{:S(2)}, u32[]{:S(2)}) collective-permute-start(f32[32,1152]{1,0:T(8,128)S(1)} %get-tuple-element.39), channel_id=1, source_target_pairs={{0,32},{4,228},{8,40},{12,236},{16,48},{20,244},{24,56},{28,252},{... | collective-permute-start | bytes 442376 | tf_op jit(solution)/shard_map/ppermute | solution.py:39
  16.4 6.3 %collective-permute-start.8 = (f32[32,1152]{1,0:T(8,128)S(1)}, f32[32,1152]{1,0:T(8,128)S(1)}, u32[]{:S(2)}, u32[]{:S(2)}) collective-permute-start(f32[32,1152]{1,0:T(8,128)S(1)} %get-tuple-element.42), channel_id=1, source_target_pairs={{0,8},{4,28},{8,0},{12,20},{16,24},{20,12},{24,16},{28,4},{32,40},... | collective-permute-start | bytes 442376 | tf_op jit(solution)/shard_map/ppermute | solution.py:39
  19.8 8.5 %collective-permute-start.4 = (f32[16,3840]{1,0:T(8,128)S(1)}, f32[16,3840]{1,0:T(8,128)S(1)}, u32[]{:S(2)}, u32[]{:S(2)}) collective-permute-start(f32[16,3840]{1,0:T(8,128)S(1)} %get-tuple-element.35), channel_id=1, source_target_pairs={{0,24},{4,12},{8,16},{12,4},{16,8},{20,28},{24,0},{28,20},{32,56},... | collective-permute-start | bytes 737288 | tf_op jit(solution)/shard_map/ppermute | solution.py:39
  22.8 7.2 %collective-permute-start.9 = (f32[16,2304]{1,0:T(8,128)S(1)}, f32[16,2304]{1,0:T(8,128)S(1)}, u32[]{:S(2)}, u32[]{:S(2)}) collective-permute-start(f32[16,2304]{1,0:T(8,128)S(1)} %get-tuple-element.45), channel_id=1, source_target_pairs={{0,24},{4,12},{8,16},{12,4},{16,8},{20,28},{24,0},{28,20},{32,56},... | collective-permute-start | bytes 442376 | tf_op jit(solution)/shard_map/ppermute | solution.py:39
  28.4 10.8 %copy-start.1 = (f32[4,6144]{1,0:T(4,128)S(1)}, f32[4,6144]{1,0:T(4,128)}, u32[]{:S(2)}) copy-start(f32[4,6144]{1,0:T(4,128)} %param.3) | copy-start | bytes 294916
  28.4 21.7 %copy-start.2 = (f32[4,6144]{1,0:T(4,128)S(1)}, f32[4,6144]{1,0:T(4,128)}, u32[]{:S(2)}) copy-start(f32[4,6144]{1,0:T(4,128)} %param.4) | copy-start | bytes 294916
  30.2 12.6 %collective-permute-start.10 = (f32[4,6144]{1,0:T(4,128)S(1)}, f32[4,6144]{1,0:T(4,128)S(1)}, u32[]{:S(2)}, u32[]{:S(2)}) collective-permute-start(f32[4,6144]{1,0:T(4,128)S(1)} %get-tuple-element.52), channel_id=1, source_target_pairs={{0,160},{4,100},{8,168},{12,108},{16,176},{20,116},{24,184},{28,12... | collective-permute-start | bytes 294920 | tf_op jit(solution)/shard_map/ppermute | solution.py:39
  35.4 7.3 %collective-permute-start.11 = (f32[4,6144]{1,0:T(4,128)S(1)}, f32[4,6144]{1,0:T(4,128)S(1)}, u32[]{:S(2)}, u32[]{:S(2)}) collective-permute-start(f32[4,6144]{1,0:T(4,128)S(1)} %get-tuple-element.46), channel_id=1, source_target_pairs={{0,192},{4,68},{8,200},{12,76},{16,208},{20,84},{24,216},{28,92},{... | collective-permute-start | bytes 294920 | tf_op jit(solution)/shard_map/ppermute | solution.py:39
  36.0 6.8 %collective-permute-start.12 = (f32[4,6144]{1,0:T(4,128)S(1)}, f32[4,6144]{1,0:T(4,128)S(1)}, u32[]{:S(2)}, u32[]{:S(2)}) collective-permute-start(f32[4,6144]{1,0:T(4,128)S(1)} %get-tuple-element.47), channel_id=1, source_target_pairs={{0,224},{4,36},{8,232},{12,44},{16,240},{20,52},{24,248},{28,60},{... | collective-permute-start | bytes 294920 | tf_op jit(solution)/shard_map/ppermute | solution.py:39
  43.0 5.2 %collective-permute-start.15 = (f32[4,2]{0,1:T(2,128)S(1)}, f32[4,2]{0,1:T(2,128)S(1)}, u32[]{:S(2)}, u32[]{:S(2)}) collective-permute-start(f32[4,2]{0,1:T(2,128)S(1)} %pad_maximum_fusion.1), channel_id=1, source_target_pairs={{0,2},{1,3},{2,0},{3,1},{4,6},{5,7},{6,4},{7,5},{8,10},{9,11},{10,... | collective-permute-start | bytes 104 | tf_op jit(solution)/shard_map/ppermute | solution.py:257
  44.3 4.8 %collective-permute-start.14 = (f32[4,2]{0,1:T(2,128)S(1)}, f32[4,2]{0,1:T(2,128)S(1)}, u32[]{:S(2)}, u32[]{:S(2)}) collective-permute-start(f32[4,2]{0,1:T(2,128)S(1)} %pad_maximum_fusion.1), channel_id=1, source_target_pairs={{0,3},{1,2},{2,1},{3,0},{4,7},{5,6},{6,5},{7,4},{8,11},{9,10},{10,... | collective-permute-start | bytes 104 | tf_op jit(solution)/shard_map/ppermute | solution.py:257
  46.5 3.6 %collective-permute-start.13 = (f32[4,2]{0,1:T(2,128)S(1)}, f32[4,2]{0,1:T(2,128)S(1)}, u32[]{:S(2)}, u32[]{:S(2)}) collective-permute-start(f32[4,2]{0,1:T(2,128)S(1)} %pad_maximum_fusion.1), channel_id=1, source_target_pairs={{0,1},{1,0},{2,3},{3,2},{4,5},{5,4},{6,7},{7,6},{8,9},{9,8},{10,11... | collective-permute-start | bytes 104 | tf_op jit(solution)/shard_map/ppermute | solution.py:257

commit v6 on v5

--- a/solution.py
+++ b/solution.py
@@ -91,15 +91,14 @@
         copies.append(pltpu.make_async_copy(src.at[pl.ds(row, 16), pl.ds(start, buf.shape[2])], buf.at[j], sem.at[j]))
     for copy in copies:
         copy.start()
-    for copy in copies:
-        copy.wait()
-
-    def body(first, n):
-        for j in range(4):
-            here = (j, slice(None), pl.ds(first, n))
-            out[here] = buf[here].astype(jnp.float32)
-
-    each_chunk(buf.shape[2], body)
+
+    def body(j, first, n):
+        here = (j, slice(None), pl.ds(first, n))
+        out[here] = buf[here].astype(jnp.float32)
+
+    for j, copy in enumerate(copies):
+        copy.wait()
+        each_chunk(buf.shape[2], functools.partial(body, j))
 
 
 def give_x_kernel(start, src, out, buf, sem):
@@ -129,18 +128,17 @@
         copies.append(pltpu.make_async_copy(src.at[pl.ds(row, 16), pl.ds(start, buf.shape[2])], buf.at[j], sem.at[j]))
     for copy in copies:
         copy.start()
-    for copy in copies:
-        copy.wait()
-
-    def body(first, n):
+
+    def body(j, first, n):
         cols = pl.ds(first, n)
         high = jnp.broadcast_to(jnp.where(x_high(x, core), 1, 0), (8, n)) == 1
-        for j in range(4):
-            rows = buf[j, :, cols].astype(jnp.float32) + got[j, :, cols]
-            own[j * 8 : j * 8 + 8, cols] = jnp.where(high, rows[8:], rows[:8])
-            out[j * 8 : j * 8 + 8, cols] = jnp.where(high, rows[:8], rows[8:])
-
-    each_chunk(buf.shape[2], body)
+        rows = buf[j, :, cols].astype(jnp.float32) + got[j, :, cols]
+        own[j * 8 : j * 8 + 8, cols] = jnp.where(high, rows[8:], rows[:8])
+        out[j * 8 : j * 8 + 8, cols] = jnp.where(high, rows[:8], rows[8:])
+
+    for j, copy in enumerate(copies):
+        copy.wait()
+        each_chunk(buf.shape[2], functools.partial(body, j))
 
 
 def a_kernel(start, src, got, own, out, buf, sem):

time: 51.6 us -> 51.7 us (level)
  transfers between devices with their start and end apart: 16 -> 16, of which waited for: 9 -> 9; matrix products, arithmetic and copies ran while one was open for 0% -> 0% of each run, Pallas kernels for 3% -> 4%
where the time goes in v6:
time: 51.7 us; the launch traced here: 51 us
  starting transfers between devices  27.6 us (53%)
  waiting for transfers between devices  18.1 us (35%)
  Pallas kernels  3.22 us (6%)
  other arithmetic  1.23 us (2%)
  between operations  0.78 us (2%)
    ppermute x13, starting transfers between devices, send(): return lax.ppermute(value, ('dp', 'row'), pairs_zx(target))  24 us
    ppermute x13, waiting for transfers between devices, send(): return lax.ppermute(value, ('dp', 'row'), pairs_zx(target))  14.6 us
    ppermute x3, starting transfers between devices, sum_over_col(): lax.ppermute(value, 'col', [(i, i ^ m) for i in range(NY)])  3.57 us
    ppermute x3, waiting for transfers between devices, sum_over_col(): lax.ppermute(value, 'col', [(i, i ^ m) for i in range(NY)])  3.5 us
    pallas_call x10, Pallas kernels, call(): pl.pallas_call(kernel, in_specs=specs, out_specs=[vmem] * len(outs), out_...  3.22 us
  transfers between devices with their start and end apart: 16, of which 9 were waited for; matrix products, arithmetic and copies ran while one was open for 0% of the time, Pallas kernels for 4%

profile of v6, /device:TPU:24, one launch (start us, length us, event | category | flops | bytes accessed | tf_op | source)
XLA Modules:
  0.0 51.0 jit_solution(820131282522787546)
XLA Ops:
  0.6 0.0 copy-start
  0.6 1.3 %shard_map.50 = f32[8,8,1920]{2,1,0:T(8,128)S(1)} custom-call(bf16[128,6144]{1,0:T(8,128)(2,1)} %bitcast.18), custom_call_target="tpu_custom_call" | custom-call | flops 1024 | bytes 1024 | tf_op jit(solution)/shard_map/pallas_call | solution.py:196
  1.9 1.6 %collective-permute-start = (f32[8,8,1920]{2,1,0:T(8,128)S(1)}, f32[8,8,1920]{2,1,0:T(8,128)S(1)}, u32[]{:S(2)}, u32[]{:S(2)}) collective-permute-start(f32[8,8,1920]{2,1,0:T(8,128)S(1)} %shard_map.50), channel_id=1, source_target_pairs={{0,8},{4,28},{8,0},{12,20},{16,24},{20,12},{24,16},{28,4},{32,40},... | collective-permute-start | bytes 1474568 | tf_op jit(solution)/shard_map/ppermute | solution.py:39
  3.5 0.0 copy-done
  3.5 0.3 shard_map.51
  3.8 2.0 %collective-permute-start.2 = (f32[4,16,1920]{2,1,0:T(8,128)S(1)}, f32[4,16,1920]{2,1,0:T(8,128)S(1)}, u32[]{:S(2)}, u32[]{:S(2)}) collective-permute-start(f32[4,16,1920]{2,1,0:T(8,128)S(1)} %shard_map.51), channel_id=1, source_target_pairs={{0,32},{4,228},{8,40},{12,236},{16,48},{20,244},{24,56},{28,252},{... | collective-permute-start | bytes 1474568 | tf_op jit(solution)/shard_map/ppermute | solution.py:39
  5.8 0.2 shard_map.52
  6.0 0.6 %collective-permute-start.5 = (f32[8,8,1152]{2,1,0:T(8,128)S(1)}, f32[8,8,1152]{2,1,0:T(8,128)S(1)}, u32[]{:S(2)}, u32[]{:S(2)}) collective-permute-start(f32[8,8,1152]{2,1,0:T(8,128)S(1)} %shard_map.52), channel_id=1, source_target_pairs={{0,8},{4,28},{8,0},{12,20},{16,24},{20,12},{24,16},{28,4},{32,40},... | collective-permute-start | bytes 884744 | tf_op jit(solution)/shard_map/ppermute | solution.py:39
  6.6 0.2 shard_map.53
  6.8 0.2 collective-permute-start.7
  7.0 3.8 %collective-permute-done.got = f32[8,8,1920]{2,1,0:T(8,128)S(1)} collective-permute-done((f32[8,8,1920]{2,1,0:T(8,128)S(1)}, f32[8,8,1920]{2,1,0:T(8,128)S(1)}, u32[]{:S(2)}, u32[]{:S(2)}) %collective-permute-start) | collective-permute-done | bytes 491552 | tf_op jit(solution)/shard_map/ppermute | solution.py:39
  10.8 0.3 shard_map.54
  11.1 2.0 %collective-permute-start.1 = (f32[32,1920]{1,0:T(8,128)S(1)}, f32[32,1920]{1,0:T(8,128)S(1)}, u32[]{:S(2)}, u32[]{:S(2)}) collective-permute-start(f32[32,1920]{1,0:T(8,128)S(1)} %get-tuple-element.30), channel_id=1, source_target_pairs={{0,32},{4,228},{8,40},{12,236},{16,48},{20,244},{24,56},{28,252},{... | collective-permute-start | bytes 737288 | tf_op jit(solution)/shard_map/ppermute | solution.py:39
  13.1 0.0 collective-permute-done.2.got
  13.1 0.4 shard_map.55
  13.5 1.6 %collective-permute-start.3 = (f32[32,1920]{1,0:T(8,128)S(1)}, f32[32,1920]{1,0:T(8,128)S(1)}, u32[]{:S(2)}, u32[]{:S(2)}) collective-permute-start(f32[32,1920]{1,0:T(8,128)S(1)} %get-tuple-element.33), channel_id=1, source_target_pairs={{0,8},{4,28},{8,0},{12,20},{16,24},{20,12},{24,16},{28,4},{32,40},... | collective-permute-start | bytes 737288 | tf_op jit(solution)/shard_map/ppermute | solution.py:39
  15.1 0.0 collective-permute-done.5.got
  15.1 0.2 shard_map.57
  15.3 0.9 %collective-permute-start.6 = (f32[32,1152]{1,0:T(8,128)S(1)}, f32[32,1152]{1,0:T(8,128)S(1)}, u32[]{:S(2)}, u32[]{:S(2)}) collective-permute-start(f32[32,1152]{1,0:T(8,128)S(1)} %get-tuple-element.39), channel_id=1, source_target_pairs={{0,32},{4,228},{8,40},{12,236},{16,48},{20,244},{24,56},{28,252},{... | collective-permute-start | bytes 442376 | tf_op jit(solution)/shard_map/ppermute | solution.py:39
  16.2 0.0 collective-permute-done.7.got
  16.2 0.2 shard_map.58
  16.4 1.6 %collective-permute-start.8 = (f32[32,1152]{1,0:T(8,128)S(1)}, f32[32,1152]{1,0:T(8,128)S(1)}, u32[]{:S(2)}, u32[]{:S(2)}) collective-permute-start(f32[32,1152]{1,0:T(8,128)S(1)} %get-tuple-element.42), channel_id=1, source_target_pairs={{0,8},{4,28},{8,0},{12,20},{16,24},{20,12},{24,16},{28,4},{32,40},... | collective-permute-start | bytes 442376 | tf_op jit(solution)/shard_map/ppermute | solution.py:39
  18.0 0.5 collective-permute-done.1.a_got
  18.5 1.3 %collective-permute-done.3.b_got = f32[32,1920]{1,0:T(8,128)S(1)} collective-permute-done((f32[32,1920]{1,0:T(8,128)S(1)}, f32[32,1920]{1,0:T(8,128)S(1)}, u32[]{:S(2)}, u32[]{:S(2)}) %collective-permute-start.3) | collective-permute-done | bytes 245792 | tf_op jit(solution)/shard_map/ppermute | solution.py:39
  19.8 0.1 shard_map.56
  19.9 2.8 %collective-permute-start.4 = (f32[16,3840]{1,0:T(8,128)S(1)}, f32[16,3840]{1,0:T(8,128)S(1)}, u32[]{:S(2)}, u32[]{:S(2)}) collective-permute-start(f32[16,3840]{1,0:T(8,128)S(1)} %get-tuple-element.35), channel_id=1, source_target_pairs={{0,24},{4,12},{8,16},{12,4},{16,8},{20,28},{24,0},{28,20},{32,56},... | collective-permute-start | bytes 737288 | tf_op jit(solution)/shard_map/ppermute | solution.py:39
  22.8 0.0 collective-permute-done.6.a_got
  22.8 0.0 collective-permute-done.8.b_got
  22.8 0.1 shard_map.59
  22.8 1.7 %collective-permute-start.9 = (f32[16,2304]{1,0:T(8,128)S(1)}, f32[16,2304]{1,0:T(8,128)S(1)}, u32[]{:S(2)}, u32[]{:S(2)}) collective-permute-start(f32[16,2304]{1,0:T(8,128)S(1)} %get-tuple-element.45), channel_id=1, source_target_pairs={{0,24},{4,12},{8,16},{12,4},{16,8},{20,28},{24,0},{28,20},{32,56},... | collective-permute-start | bytes 442376 | tf_op jit(solution)/shard_map/ppermute | solution.py:39
  24.6 4.0 %collective-permute-done.4 = f32[16,3840]{1,0:T(8,128)S(1)} collective-permute-done((f32[16,3840]{1,0:T(8,128)S(1)}, f32[16,3840]{1,0:T(8,128)S(1)}, u32[]{:S(2)}, u32[]{:S(2)}) %collective-permute-start.4) | collective-permute-done | bytes 245792 | tf_op jit(solution)/shard_map/ppermute | solution.py:39
  28.5 0.0 copy-start.1
  28.6 0.0 copy-start.2
  28.6 1.5 %collective-permute-done.9 = f32[16,2304]{1,0:T(8,128)S(1)} collective-permute-done((f32[16,2304]{1,0:T(8,128)S(1)}, f32[16,2304]{1,0:T(8,128)S(1)}, u32[]{:S(2)}, u32[]{:S(2)}) %collective-permute-start.9) | collective-permute-done | bytes 147488 | tf_op jit(solution)/shard_map/ppermute | solution.py:39
  30.2 0.1 reshape.7
  30.3 5.3 %collective-permute-start.10 = (f32[4,6144]{1,0:T(4,128)S(1)}, f32[4,6144]{1,0:T(4,128)S(1)}, u32[]{:S(2)}, u32[]{:S(2)}) collective-permute-start(f32[4,6144]{1,0:T(4,128)S(1)} %get-tuple-element.52), channel_id=1, source_target_pairs={{0,160},{4,100},{8,168},{12,108},{16,176},{20,116},{24,184},{28,12... | collective-permute-start | bytes 294920 | tf_op jit(solution)/shard_map/ppermute | solution.py:39
  35.6 0.6 %collective-permute-start.11 = (f32[4,6144]{1,0:T(4,128)S(1)}, f32[4,6144]{1,0:T(4,128)S(1)}, u32[]{:S(2)}, u32[]{:S(2)}) collective-permute-start(f32[4,6144]{1,0:T(4,128)S(1)} %get-tuple-element.46), channel_id=1, source_target_pairs={{0,192},{4,68},{8,200},{12,76},{16,208},{20,84},{24,216},{28,92},{... | collective-permute-start | bytes 294920 | tf_op jit(solution)/shard_map/ppermute | solution.py:39
  36.1 3.1 %collective-permute-start.12 = (f32[4,6144]{1,0:T(4,128)S(1)}, f32[4,6144]{1,0:T(4,128)S(1)}, u32[]{:S(2)}, u32[]{:S(2)}) collective-permute-start(f32[4,6144]{1,0:T(4,128)S(1)} %get-tuple-element.47), channel_id=1, source_target_pairs={{0,224},{4,36},{8,232},{12,44},{16,240},{20,52},{24,248},{28,60},{... | collective-permute-start | bytes 294920 | tf_op jit(solution)/shard_map/ppermute | solution.py:39
  39.3 0.0 copy-done.1
  39.3 0.2 multiply_reduce_fusion.1
  39.4 3.5 %collective-permute-done.12 = f32[4,6144]{1,0:T(4,128)S(1)} collective-permute-done((f32[4,6144]{1,0:T(4,128)S(1)}, f32[4,6144]{1,0:T(4,128)S(1)}, u32[]{:S(2)}, u32[]{:S(2)}) %collective-permute-start.12) | collective-permute-done | bytes 98336 | tf_op jit(solution)/shard_map/ppermute | solution.py:39
  42.9 0.0 collective-permute-done.11
  42.9 0.0 collective-permute-done.10
  42.9 0.2 multiply_reduce_fusion
  43.1 1.3 %collective-permute-start.15 = (f32[4,2]{0,1:T(2,128)S(1)}, f32[4,2]{0,1:T(2,128)S(1)}, u32[]{:S(2)}, u32[]{:S(2)}) collective-permute-start(f32[4,2]{0,1:T(2,128)S(1)} %pad_maximum_fusion.1), channel_id=1, source_target_pairs={{0,2},{1,3},{2,0},{3,1},{4,6},{5,7},{6,4},{7,5},{8,10},{9,11},{10,... | collective-permute-start | bytes 104 | tf_op jit(solution)/shard_map/ppermute | solution.py:255
  44.4 2.2 %collective-permute-start.14 = (f32[4,2]{0,1:T(2,128)S(1)}, f32[4,2]{0,1:T(2,128)S(1)}, u32[]{:S(2)}, u32[]{:S(2)}) collective-permute-start(f32[4,2]{0,1:T(2,128)S(1)} %pad_maximum_fusion.1), channel_id=1, source_target_pairs={{0,3},{1,2},{2,1},{3,0},{4,7},{5,6},{6,5},{7,4},{8,11},{9,10},{10,... | collective-permute-start | bytes 104 | tf_op jit(solution)/shard_map/ppermute | solution.py:255
  46.6 0.1 collective-permute-start.13
  46.7 1.6 %collective-permute-done.15 = f32[4,2]{0,1:T(2,128)S(1)} collective-permute-done((f32[4,2]{0,1:T(2,128)S(1)}, f32[4,2]{0,1:T(2,128)S(1)}, u32[]{:S(2)}, u32[]{:S(2)}) %collective-permute-start.15) | collective-permute-done | bytes 64 | tf_op jit(solution)/shard_map/ppermute | solution.py:255
  48.3 0.9 %collective-permute-done.14 = f32[4,2]{0,1:T(2,128)S(1)} collective-permute-done((f32[4,2]{0,1:T(2,128)S(1)}, f32[4,2]{0,1:T(2,128)S(1)}, u32[]{:S(2)}, u32[]{:S(2)}) %collective-permute-start.14) | collective-permute-done | bytes 64 | tf_op jit(solution)/shard_map/ppermute | solution.py:255
  49.2 1.0 %collective-permute-done.13 = f32[4,2]{0,1:T(2,128)S(1)} collective-permute-done((f32[4,2]{0,1:T(2,128)S(1)}, f32[4,2]{0,1:T(2,128)S(1)}, u32[]{:S(2)}, u32[]{:S(2)}) %collective-permute-start.13) | collective-permute-done | bytes 64 | tf_op jit(solution)/shard_map/ppermute | solution.py:255
  50.2 0.0 copy-done.2
  50.2 0.8 %fusion.2 = (f32[4,6144]{1,0:T(4,128)}, f32[4,6144]{1,0:T(4,128)}) fusion(f32[4,6144]{1,0:T(4,128)S(1)} %copy-done.1, f32[4,6144]{1,0:T(4,128)S(1)} %get-tuple-element.51, f32[4]{0:T(128)S(1)} %minimum_bitcast_fusion, f32[4,6144]{1,0:T(4,128)S(1)} %copy-done.2), kind=kLoop, calls=%fused_computation.13 | loop fusion | flops 98304 | bytes 491536 | tf_op jit(solution)/shard_map/sub | solution.py:266
  (7 shorter events, 0.1 us)
Async XLA Ops:
  0.6 2.9 %copy-start = (bf16[1,128,6144]{2,1,0:T(8,128)(2,1)S(1)}, bf16[1,128,6144]{2,1,0:T(8,128)(2,1)}, u32[]{:S(2)}) copy-start(bf16[1,128,6144]{2,1,0:T(8,128)(2,1)} %param.5) | copy-start | bytes 4718596
  1.9 8.9 %collective-permute-start = (f32[8,8,1920]{2,1,0:T(8,128)S(1)}, f32[8,8,1920]{2,1,0:T(8,128)S(1)}, u32[]{:S(2)}, u32[]{:S(2)}) collective-permute-start(f32[8,8,1920]{2,1,0:T(8,128)S(1)} %shard_map.50), channel_id=1, source_target_pairs={{0,8},{4,28},{8,0},{12,20},{16,24},{20,12},{24,16},{28,4},{32,40},... | collective-permute-start | bytes 1474568 | tf_op jit(solution)/shard_map/ppermute | solution.py:39
  3.8 9.3 %collective-permute-start.2 = (f32[4,16,1920]{2,1,0:T(8,128)S(1)}, f32[4,16,1920]{2,1,0:T(8,128)S(1)}, u32[]{:S(2)}, u32[]{:S(2)}) collective-permute-start(f32[4,16,1920]{2,1,0:T(8,128)S(1)} %shard_map.51), channel_id=1, source_target_pairs={{0,32},{4,228},{8,40},{12,236},{16,48},{20,244},{24,56},{28,252},{... | collective-permute-start | bytes 1474568 | tf_op jit(solution)/shard_map/ppermute | solution.py:39
  6.0 9.1 %collective-permute-start.5 = (f32[8,8,1152]{2,1,0:T(8,128)S(1)}, f32[8,8,1152]{2,1,0:T(8,128)S(1)}, u32[]{:S(2)}, u32[]{:S(2)}) collective-permute-start(f32[8,8,1152]{2,1,0:T(8,128)S(1)} %shard_map.52), channel_id=1, source_target_pairs={{0,8},{4,28},{8,0},{12,20},{16,24},{20,12},{24,16},{28,4},{32,40},... | collective-permute-start | bytes 884744 | tf_op jit(solution)/shard_map/ppermute | solution.py:39
  6.8 9.4 %collective-permute-start.7 = (f32[4,16,1152]{2,1,0:T(8,128)S(1)}, f32[4,16,1152]{2,1,0:T(8,128)S(1)}, u32[]{:S(2)}, u32[]{:S(2)}) collective-permute-start(f32[4,16,1152]{2,1,0:T(8,128)S(1)} %shard_map.53), channel_id=1, source_target_pairs={{0,32},{4,228},{8,40},{12,236},{16,48},{20,244},{24,56},{28,252},{... | collective-permute-start | bytes 884744 | tf_op jit(solution)/shard_map/ppermute | solution.py:39
  11.1 7.4 %collective-permute-start.1 = (f32[32,1920]{1,0:T(8,128)S(1)}, f32[32,1920]{1,0:T(8,128)S(1)}, u32[]{:S(2)}, u32[]{:S(2)}) collective-permute-start(f32[32,1920]{1,0:T(8,128)S(1)} %get-tuple-element.30), channel_id=1, source_target_pairs={{0,32},{4,228},{8,40},{12,236},{16,48},{20,244},{24,56},{28,252},{... | collective-permute-start | bytes 737288 | tf_op jit(solution)/shard_map/ppermute | solution.py:39
  13.5 6.3 %collective-permute-start.3 = (f32[32,1920]{1,0:T(8,128)S(1)}, f32[32,1920]{1,0:T(8,128)S(1)}, u32[]{:S(2)}, u32[]{:S(2)}) collective-permute-start(f32[32,1920]{1,0:T(8,128)S(1)} %get-tuple-element.33), channel_id=1, source_target_pairs={{0,8},{4,28},{8,0},{12,20},{16,24},{20,12},{24,16},{28,4},{32,40},... | collective-permute-start | bytes 737288 | tf_op jit(solution)/shard_map/ppermute | solution.py:39
  15.3 7.5 %collective-permute-start.6 = (f32[32,1152]{1,0:T(8,128)S(1)}, f32[32,1152]{1,0:T(8,128)S(1)}, u32[]{:S(2)}, u32[]{:S(2)}) collective-permute-start(f32[32,1152]{1,0:T(8,128)S(1)} %get-tuple-element.39), channel_id=1, source_target_pairs={{0,32},{4,228},{8,40},{12,236},{16,48},{20,244},{24,56},{28,252},{... | collective-permute-start | bytes 442376 | tf_op jit(solution)/shard_map/ppermute | solution.py:39
  16.4 6.3 %collective-permute-start.8 = (f32[32,1152]{1,0:T(8,128)S(1)}, f32[32,1152]{1,0:T(8,128)S(1)}, u32[]{:S(2)}, u32[]{:S(2)}) collective-permute-start(f32[32,1152]{1,0:T(8,128)S(1)} %get-tuple-element.42), channel_id=1, source_target_pairs={{0,8},{4,28},{8,0},{12,20},{16,24},{20,12},{24,16},{28,4},{32,40},... | collective-permute-start | bytes 442376 | tf_op jit(solution)/shard_map/ppermute | solution.py:39
  19.9 8.6 %collective-permute-start.4 = (f32[16,3840]{1,0:T(8,128)S(1)}, f32[16,3840]{1,0:T(8,128)S(1)}, u32[]{:S(2)}, u32[]{:S(2)}) collective-permute-start(f32[16,3840]{1,0:T(8,128)S(1)} %get-tuple-element.35), channel_id=1, source_target_pairs={{0,24},{4,12},{8,16},{12,4},{16,8},{20,28},{24,0},{28,20},{32,56},... | collective-permute-start | bytes 737288 | tf_op jit(solution)/shard_map/ppermute | solution.py:39
  22.8 7.3 %collective-permute-start.9 = (f32[16,2304]{1,0:T(8,128)S(1)}, f32[16,2304]{1,0:T(8,128)S(1)}, u32[]{:S(2)}, u32[]{:S(2)}) collective-permute-start(f32[16,2304]{1,0:T(8,128)S(1)} %get-tuple-element.45), channel_id=1, source_target_pairs={{0,24},{4,12},{8,16},{12,4},{16,8},{20,28},{24,0},{28,20},{32,56},... | collective-permute-start | bytes 442376 | tf_op jit(solution)/shard_map/ppermute | solution.py:39
  28.5 10.7 %copy-start.1 = (f32[4,6144]{1,0:T(4,128)S(1)}, f32[4,6144]{1,0:T(4,128)}, u32[]{:S(2)}) copy-start(f32[4,6144]{1,0:T(4,128)} %param.3) | copy-start | bytes 294916
  28.6 21.7 %copy-start.2 = (f32[4,6144]{1,0:T(4,128)S(1)}, f32[4,6144]{1,0:T(4,128)}, u32[]{:S(2)}) copy-start(f32[4,6144]{1,0:T(4,128)} %param.4) | copy-start | bytes 294916
  30.3 12.6 %collective-permute-start.10 = (f32[4,6144]{1,0:T(4,128)S(1)}, f32[4,6144]{1,0:T(4,128)S(1)}, u32[]{:S(2)}, u32[]{:S(2)}) collective-permute-start(f32[4,6144]{1,0:T(4,128)S(1)} %get-tuple-element.52), channel_id=1, source_target_pairs={{0,160},{4,100},{8,168},{12,108},{16,176},{20,116},{24,184},{28,12... | collective-permute-start | bytes 294920 | tf_op jit(solution)/shard_map/ppermute | solution.py:39
  35.6 7.3 %collective-permute-start.11 = (f32[4,6144]{1,0:T(4,128)S(1)}, f32[4,6144]{1,0:T(4,128)S(1)}, u32[]{:S(2)}, u32[]{:S(2)}) collective-permute-start(f32[4,6144]{1,0:T(4,128)S(1)} %get-tuple-element.46), channel_id=1, source_target_pairs={{0,192},{4,68},{8,200},{12,76},{16,208},{20,84},{24,216},{28,92},{... | collective-permute-start | bytes 294920 | tf_op jit(solution)/shard_map/ppermute | solution.py:39
  36.1 6.8 %collective-permute-start.12 = (f32[4,6144]{1,0:T(4,128)S(1)}, f32[4,6144]{1,0:T(4,128)S(1)}, u32[]{:S(2)}, u32[]{:S(2)}) collective-permute-start(f32[4,6144]{1,0:T(4,128)S(1)} %get-tuple-element.47), channel_id=1, source_target_pairs={{0,224},{4,36},{8,232},{12,44},{16,240},{20,52},{24,248},{28,60},{... | collective-permute-start | bytes 294920 | tf_op jit(solution)/shard_map/ppermute | solution.py:39
  43.1 5.2 %collective-permute-start.15 = (f32[4,2]{0,1:T(2,128)S(1)}, f32[4,2]{0,1:T(2,128)S(1)}, u32[]{:S(2)}, u32[]{:S(2)}) collective-permute-start(f32[4,2]{0,1:T(2,128)S(1)} %pad_maximum_fusion.1), channel_id=1, source_target_pairs={{0,2},{1,3},{2,0},{3,1},{4,6},{5,7},{6,4},{7,5},{8,10},{9,11},{10,... | collective-permute-start | bytes 104 | tf_op jit(solution)/shard_map/ppermute | solution.py:255
  44.4 4.8 %collective-permute-start.14 = (f32[4,2]{0,1:T(2,128)S(1)}, f32[4,2]{0,1:T(2,128)S(1)}, u32[]{:S(2)}, u32[]{:S(2)}) collective-permute-start(f32[4,2]{0,1:T(2,128)S(1)} %pad_maximum_fusion.1), channel_id=1, source_target_pairs={{0,3},{1,2},{2,1},{3,0},{4,7},{5,6},{6,5},{7,4},{8,11},{9,10},{10,... | collective-permute-start | bytes 104 | tf_op jit(solution)/shard_map/ppermute | solution.py:255
  46.6 3.6 %collective-permute-start.13 = (f32[4,2]{0,1:T(2,128)S(1)}, f32[4,2]{0,1:T(2,128)S(1)}, u32[]{:S(2)}, u32[]{:S(2)}) collective-permute-start(f32[4,2]{0,1:T(2,128)S(1)} %pad_maximum_fusion.1), channel_id=1, source_target_pairs={{0,1},{1,0},{2,3},{3,2},{4,5},{5,4},{6,7},{7,6},{8,9},{9,8},{10,11... | collective-permute-start | bytes 104 | tf_op jit(solution)/shard_map/ppermute | solution.py:255
